TPU v7x, 512 devices: a whole 4x8x8 slice. The times are simulated.
512 devices in a mesh: pipe: 16 (over z_lo, x), ctx: 16 (over y, z_hi), head: 2 (over core).
Axes of the slice: x: 4, y: 8, z: 8 (z_hi: 2, z_lo: 4; z = z_hi * 4 + z_lo), core: 2. Of those that a mesh axis runs over, the one named last changes fastest.
Arguments:
- queries: bfloat16 [16, 2048, 64, 128], P('pipe', 'ctx', 'head'), may hold values from -160 to 160
- key_heads: bfloat16 [16, 2048, 8, 128], P('pipe', 'ctx', 'head'), may hold values from -6 to 6
- value_heads: bfloat16 [16, 2048, 8, 128], P('pipe', 'ctx', 'head'), may hold values from -6 to 6
- forward_out: bfloat16 [16, 2048, 64, 128], P('pipe', 'ctx', 'head'), may hold values from -4 to 4
- output_grad: bfloat16 [16, 2048, 64, 128], P('pipe', 'ctx', 'head'), may hold values from -6 to 6
- block_order: int32 [32], replicated, may hold values from 0 to 31, each once
Outputs:
- key_grad: bfloat16 [16, 2048, 8, 128], P('pipe', 'ctx', 'head')
- value_grad: bfloat16 [16, 2048, 8, 128], P('pipe', 'ctx', 'head')
- handed: bfloat16 [16, 2048, 64, 128], P('pipe', 'ctx', 'head')
Inputs may be any that keep to these rules, and one draw needn't show every extreme that they name: `block_order`: every half-block number appears exactly once.
All inputs are finite; a program needn't handle non-finite values.
Results may differ from a plain program's by a relative error of at most 0.012.
The roundings to bfloat16 on the way count: a program that leaves them out, or rounds other values in their place, can miss the bound.
Values may be sent and summed in bfloat16 or wider, within the bound.
A program may use at most 64 MiB of HBM per device.

v0:
```python
import math

import jax
import jax.numpy as jnp
from jax import lax
from jax.sharding import PartitionSpec as P

NEG = -1e30


def passed_along(value, axis, steps):
    count = lax.axis_size(axis)
    pairs = [(source, (source + steps) % count) for source in range(count)]
    return lax.ppermute(value, axis, pairs)


def shifted(value, axis, steps):
    count = lax.axis_size(axis)
    first, last = (max(0, -steps), min(count, count - steps))
    return lax.ppermute(value, axis, [(source, source + steps) for source in range(first, last)])


def hadamard(size_in):
    indices = jnp.arange(size_in, dtype=jnp.int32)
    parity = jnp.zeros((size_in, size_in), jnp.int32)
    for bit_place in range(size_in.bit_length() - 1):
        digit = indices // 2**bit_place % 2
        parity = parity + digit[:, None] * digit[None, :]
    parity = parity % 2
    return (1.0 - 2.0 * parity.astype(jnp.float32)) / math.sqrt(size_in)


def rotate(values, rotation):
    return jnp.dot(values.astype(jnp.float32), rotation, precision=lax.Precision.HIGHEST).astype(
        jnp.bfloat16
    )


def half_starts(block_order, source):
    return lax.dynamic_slice_in_dim(block_order, source * 2, 2)


def stat_update(running, q_rows, q_pos, k_rows, k_pos, score_scale):
    row_top, row_total = running
    scores = (
        jnp.einsum("iagd,jad->agij", q_rows, k_rows, preferred_element_type=jnp.float32)
        * score_scale
    )
    visible = k_pos[None, :] <= q_pos[:, None]
    scores = jnp.where(visible, scores, NEG)
    new_top = jnp.maximum(row_top, jnp.max(scores, -1))
    weight = jnp.where(visible, jnp.exp(scores - new_top[..., None]), 0.0)
    row_total = row_total * jnp.exp(row_top - new_top) + jnp.sum(weight, -1)
    return (new_top, row_total)


def pair_grads(q_rows, g_rows, lse_rows, delta_rows, q_pos, k_rows, v_rows, k_pos, score_scale):
    scores = (
        jnp.einsum("iagd,jad->agij", q_rows, k_rows, preferred_element_type=jnp.float32)
        * score_scale
    )
    visible = k_pos[None, :] <= q_pos[:, None]
    scores = jnp.where(visible, scores, NEG)
    weights = jnp.exp(scores - lse_rows[..., None])
    weight_grad = jnp.einsum("iagd,jad->agij", g_rows, v_rows, preferred_element_type=jnp.float32)
    dscore = (weights * (weight_grad - delta_rows[..., None])).astype(jnp.bfloat16)
    weights_low = weights.astype(jnp.bfloat16)
    dq_part = jnp.einsum("agij,jad->iagd", dscore, k_rows, preferred_element_type=jnp.float32)
    dk_part = jnp.einsum("agij,iagd->jad", dscore, q_rows, preferred_element_type=jnp.float32)
    dv_part = jnp.einsum("agij,iagd->jad", weights_low, g_rows, preferred_element_type=jnp.float32)
    return (dq_part, dk_part, dv_part)


def keep_sums(sums):
    return sums


def shards(queries, key_heads, value_heads, forward_out, output_grad, block_order):
    head_size = queries.shape[-1]
    tok_rows = queries.shape[1]
    half_rows = tok_rows // 2
    kv_groups = key_heads.shape[2]
    q_heads = queries.shape[2]
    per_group = q_heads // kv_groups
    rotation = hadamard(head_size)
    score_scale = 1.0 / math.sqrt(head_size)
    cycle_size = lax.axis_size("ctx")
    cycle_place = lax.axis_index("ctx")
    q_rot = rotate(queries[0], rotation).reshape(tok_rows, kv_groups, per_group, head_size)
    k_rot = rotate(key_heads[0], rotation)
    v_heads = value_heads[0]
    grad_out = output_grad[0].reshape(tok_rows, kv_groups, per_group, head_size)
    saved_out = forward_out[0].reshape(tok_rows, kv_groups, per_group, head_size)
    row_delta = jnp.transpose(
        jnp.sum(grad_out.astype(jnp.float32) * saved_out.astype(jnp.float32), -1), (1, 2, 0)
    )
    offsets = jnp.arange(half_rows, dtype=jnp.int32)
    q_starts = half_starts(block_order, cycle_place)
    q_pos = (q_starts[:, None] * half_rows + offsets[None, :]).reshape(tok_rows)
    top_init = jnp.full((kv_groups, per_group, tok_rows), NEG, jnp.float32)
    total_init = jnp.zeros((kv_groups, per_group, tok_rows), jnp.float32)

    def absorb_stats(running, k_block, source):
        k_starts = half_starts(block_order, source)
        for k_half in range(2):
            k_pos = k_starts[k_half] * half_rows + offsets
            k_piece = k_block[k_half * half_rows : (k_half + 1) * half_rows]

            def apply_stats(carried, k_piece=k_piece, k_pos=k_pos):
                return stat_update(carried, q_rot, q_pos, k_piece, k_pos, score_scale)

            running = lax.cond(
                k_starts[k_half] <= jnp.max(q_starts), apply_stats, keep_sums, running
            )
        return running

    row_stats = absorb_stats((top_init, total_init), k_rot, cycle_place)

    def stat_step(hop_index, loop_state):
        running, k_block = loop_state
        k_block = passed_along(k_block, "ctx", 1)
        running = absorb_stats(running, k_block, (cycle_place - hop_index) % cycle_size)
        return (running, k_block)

    row_stats, last_block = lax.fori_loop(1, cycle_size, stat_step, (row_stats, k_rot))
    row_lse = row_stats[0] + jnp.log(row_stats[1])

    def absorb_grads(dq_sum, kv_block, sum_block, first_group, source):
        k_block, v_block = kv_block
        dk_sum, dv_sum = sum_block
        width = k_block.shape[1]
        last_group = first_group + width
        k_starts = half_starts(block_order, source)
        sums = (dq_sum, dk_sum, dv_sum)
        for q_half in range(2):
            for k_half in range(2):

                def apply_pair(carried, q_half=q_half, k_half=k_half):
                    dq_acc, dk_acc, dv_acc = carried
                    q_lo = q_half * half_rows
                    k_lo = k_half * half_rows
                    k_pos = k_starts[k_half] * half_rows + offsets
                    parts = pair_grads(
                        q_rot[q_lo : q_lo + half_rows, first_group:last_group],
                        grad_out[q_lo : q_lo + half_rows, first_group:last_group],
                        row_lse[first_group:last_group, :, q_lo : q_lo + half_rows],
                        row_delta[first_group:last_group, :, q_lo : q_lo + half_rows],
                        q_pos[q_lo : q_lo + half_rows],
                        k_block[k_lo : k_lo + half_rows],
                        v_block[k_lo : k_lo + half_rows],
                        k_pos,
                        score_scale,
                    )
                    dq_acc = dq_acc.at[q_lo : q_lo + half_rows, first_group:last_group].add(
                        parts[0]
                    )
                    dk_acc = dk_acc.at[k_lo : k_lo + half_rows].add(parts[1])
                    dv_acc = dv_acc.at[k_lo : k_lo + half_rows].add(parts[2])
                    return (dq_acc, dk_acc, dv_acc)

                sums = lax.cond(k_starts[k_half] <= q_starts[q_half], apply_pair, keep_sums, sums)
        return (sums[0], (sums[1], sums[2]))

    dq_init = jnp.zeros((tok_rows, kv_groups, per_group, head_size), jnp.float32)
    acc_zero = jnp.zeros((tok_rows, kv_groups, head_size), jnp.float32)

    def cycle_step(hop_index, loop_state):
        dq_sum, kv_block, sum_block = loop_state
        dq_sum, sum_block = absorb_grads(
            dq_sum, kv_block, sum_block, 0, (cycle_place - hop_index) % cycle_size
        )
        kv_block = passed_along((kv_block[0], kv_block[1]), "ctx", 1)
        sum_block = passed_along((sum_block[0], sum_block[1]), "ctx", 1)
        return (dq_sum, kv_block, sum_block)

    dq_sum, kv_block, sum_block = lax.fori_loop(
        0, cycle_size, cycle_step, (dq_init, (k_rot, v_heads), (acc_zero, acc_zero))
    )
    dk_sum, dv_sum = sum_block
    dq_full = jnp.dot(
        (dq_sum * score_scale).reshape(-1, head_size), rotation.T, precision=lax.Precision.HIGHEST
    )
    dk_full = jnp.dot(
        (dk_sum * score_scale).reshape(-1, head_size), rotation.T, precision=lax.Precision.HIGHEST
    )
    key_grad = dk_full.reshape(1, tok_rows, kv_groups, head_size).astype(jnp.bfloat16)
    value_grad = dv_sum.reshape(1, tok_rows, kv_groups, head_size).astype(jnp.bfloat16)
    handed_local = (grad_out.astype(jnp.float32).reshape(-1, head_size) + dq_full).astype(
        jnp.bfloat16
    )
    handed_local = handed_local.reshape(1, tok_rows, q_heads, head_size)
    handed = shifted(handed_local, "pipe", -1)
    return (key_grad, value_grad, handed)


def solution(mesh):
    placed = (
        P("pipe", "ctx", "head", None),
        P("pipe", "ctx", "head", None),
        P("pipe", "ctx", "head", None),
        P("pipe", "ctx", "head", None),
        P("pipe", "ctx", "head", None),
        P(),
    )
    return jax.shard_map(
        shards,
        mesh=mesh,
        in_specs=placed,
        out_specs=(
            P("pipe", "ctx", "head", None),
            P("pipe", "ctx", "head", None),
            P("pipe", "ctx", "head", None),
        ),
        check_vma=False,
    )
```

profile of v0, /device:TPU:104, one launch (start us, length us, event | category | flops | bytes accessed | tf_op | source)
XLA Modules:
  0.0 1494.0 jit_solution(9619993212502191934)
XLA Ops:
  29.9 270.4 %while.58 = (s32[]{:T(128)}, f32[4,8,128]{2,1,0:T(8,128)}, f32[4,8,128]{2,1,0:T(8,128)S(1)}, bf16[128,4,128]{2,0,1:T(8,128)(2,1)S(1)}, s32[]{:T(128)}, /*index=5...) while((s32[]{:T(128)}, f32[4,8,128]{2,1,0:T(8,128)}, ...), condition=%wide.region_18.19_spmd.clone.clone, body=%wide.region_9.18_spmd.clone.clone.sunk | while | flops 137396512 | bytes 7820916 | solution.py:125
  29.9 10.0 collective-permute-start
  138.2 7.1 collective-permute-start
  175.6 9.2 collective-permute-start
  229.7 9.9 collective-permute-start
  304.0 1167.2 %while.59 = (s32[]{:T(128)}, f32[128,4,8,128]{3,0,2,1:T(8,128)}, bf16[128,4,128]{2,0,1:T(8,128)(2,1)}, bf16[128,4,128]{2,0,1:T(8,128)(2,1)}, f32[128,4,128]{2,0,...) while((s32[]{:T(128)}, f32[128,4,8,128]{3,0,2,1:T(8,128)}, ...), condition=%wide.region_29.30_spmd.clone.clone, body=%wide.region_20.29_spmd.clone.clone.sunk | while | flops 676086144 | bytes 50848100 | solution.py:176
  315.7 7.4 conditional.30
  323.0 8.3 conditional.32
  331.4 9.6 conditional.33
  341.0 6.4 collective-permute-start.3
  347.4 12.5 collective-permute-start.4
  385.5 8.3 conditional.32
  393.8 9.6 conditional.33
  409.1 22.6 %collective-permute-start.4 = (f32[128,4,128]{2,0,1:T(8,128)S(1)}, f32[128,4,128]{2,0,1:T(8,128)}, u32[]{:S(2)}, u32[]{:S(2)}) collective-permute-start(f32[128,4,128]{2,0,1:T(8,128)S(1)} %get-tuple-element.1613), channel_id=1, source_target_pairs={{0,2},{2,4},{4,6},{6,8},{8,10},{10,12},{12,14},{14,16},{16,18},{18... | collective-permute-start | bytes 786440 | tf_op jit(solution)/shard_map/while/body/eval_jaxpr/ppermute | solution.py:14
  457.2 8.3 conditional.32
  465.5 9.6 conditional.33
  475.1 23.1 %collective-permute-start.3 = (f32[128,4,128]{2,0,1:T(8,128)}, f32[128,4,128]{2,0,1:T(8,128)}, u32[]{:S(2)}, u32[]{:S(2)}) collective-permute-start(f32[128,4,128]{2,0,1:T(8,128)} %get-tuple-element.1612), channel_id=1, source_target_pairs={{0,2},{2,4},{4,6},{6,8},{8,10},{10,12},{12,14},{14,16},{16,18},{18... | collective-permute-start | bytes 786440 | tf_op jit(solution)/shard_map/while/body/eval_jaxpr/ppermute | solution.py:14
  530.0 8.3 conditional.32
  538.3 9.6 conditional.33
  547.9 24.4 %collective-permute-start.3 = (f32[128,4,128]{2,0,1:T(8,128)}, f32[128,4,128]{2,0,1:T(8,128)}, u32[]{:S(2)}, u32[]{:S(2)}) collective-permute-start(f32[128,4,128]{2,0,1:T(8,128)} %get-tuple-element.1612), channel_id=1, source_target_pairs={{0,2},{2,4},{4,6},{6,8},{8,10},{10,12},{12,14},{14,16},{16,18},{18... | collective-permute-start | bytes 786440 | tf_op jit(solution)/shard_map/while/body/eval_jaxpr/ppermute | solution.py:14
  605.1 8.3 conditional.32
  613.4 9.6 conditional.33
  628.1 18.5 %collective-permute-start.4 = (f32[128,4,128]{2,0,1:T(8,128)S(1)}, f32[128,4,128]{2,0,1:T(8,128)}, u32[]{:S(2)}, u32[]{:S(2)}) collective-permute-start(f32[128,4,128]{2,0,1:T(8,128)S(1)} %get-tuple-element.1613), channel_id=1, source_target_pairs={{0,2},{2,4},{4,6},{6,8},{8,10},{10,12},{12,14},{14,16},{16,18},{18... | collective-permute-start | bytes 786440 | tf_op jit(solution)/shard_map/while/body/eval_jaxpr/ppermute | solution.py:14
  674.7 9.6 conditional.33
  684.3 14.6 collective-permute-start.3
  698.9 19.8 %collective-permute-start.4 = (f32[128,4,128]{2,0,1:T(8,128)S(1)}, f32[128,4,128]{2,0,1:T(8,128)}, u32[]{:S(2)}, u32[]{:S(2)}) collective-permute-start(f32[128,4,128]{2,0,1:T(8,128)S(1)} %get-tuple-element.1613), channel_id=1, source_target_pairs={{0,2},{2,4},{4,6},{6,8},{8,10},{10,12},{12,14},{14,16},{16,18},{18... | collective-permute-start | bytes 786440 | tf_op jit(solution)/shard_map/while/body/eval_jaxpr/ppermute | solution.py:14
  748.7 8.3 conditional.32
  757.0 6.9 collective-permute-start.3
  763.9 27.3 %collective-permute-start.4 = (f32[128,4,128]{2,0,1:T(8,128)S(1)}, f32[128,4,128]{2,0,1:T(8,128)}, u32[]{:S(2)}, u32[]{:S(2)}) collective-permute-start(f32[128,4,128]{2,0,1:T(8,128)S(1)} %get-tuple-element.1613), channel_id=1, source_target_pairs={{0,2},{2,4},{4,6},{6,8},{8,10},{10,12},{12,14},{14,16},{16,18},{18... | collective-permute-start | bytes 786440 | tf_op jit(solution)/shard_map/while/body/eval_jaxpr/ppermute | solution.py:14
  806.8 7.9 collective-permute-done.2
  826.3 8.3 conditional.32
  834.6 9.6 conditional.33
  848.1 20.2 %collective-permute-start.4 = (f32[128,4,128]{2,0,1:T(8,128)S(1)}, f32[128,4,128]{2,0,1:T(8,128)}, u32[]{:S(2)}, u32[]{:S(2)}) collective-permute-start(f32[128,4,128]{2,0,1:T(8,128)S(1)} %get-tuple-element.1613), channel_id=1, source_target_pairs={{0,2},{2,4},{4,6},{6,8},{8,10},{10,12},{12,14},{14,16},{16,18},{18... | collective-permute-start | bytes 786440 | tf_op jit(solution)/shard_map/while/body/eval_jaxpr/ppermute | solution.py:14
  868.3 7.8 collective-permute-start.1
  902.2 8.3 conditional.32
  910.5 9.6 conditional.33
  920.2 15.6 %collective-permute-start.3 = (f32[128,4,128]{2,0,1:T(8,128)}, f32[128,4,128]{2,0,1:T(8,128)}, u32[]{:S(2)}, u32[]{:S(2)}) collective-permute-start(f32[128,4,128]{2,0,1:T(8,128)} %get-tuple-element.1612), channel_id=1, source_target_pairs={{0,2},{2,4},{4,6},{6,8},{8,10},{10,12},{12,14},{14,16},{16,18},{18... | collective-permute-start | bytes 786440 | tf_op jit(solution)/shard_map/while/body/eval_jaxpr/ppermute | solution.py:14
  935.8 7.2 collective-permute-start.4
  973.1 8.3 conditional.32
  981.4 9.6 conditional.33
  991.0 13.8 collective-permute-start.3
  1004.8 16.1 %collective-permute-start.4 = (f32[128,4,128]{2,0,1:T(8,128)S(1)}, f32[128,4,128]{2,0,1:T(8,128)}, u32[]{:S(2)}, u32[]{:S(2)}) collective-permute-start(f32[128,4,128]{2,0,1:T(8,128)S(1)} %get-tuple-element.1613), channel_id=1, source_target_pairs={{0,2},{2,4},{4,6},{6,8},{8,10},{10,12},{12,14},{14,16},{16,18},{18... | collective-permute-start | bytes 786440 | tf_op jit(solution)/shard_map/while/body/eval_jaxpr/ppermute | solution.py:14
  1046.6 8.3 conditional.32
  1054.9 9.6 conditional.33
  1066.5 30.3 %collective-permute-start.4 = (f32[128,4,128]{2,0,1:T(8,128)S(1)}, f32[128,4,128]{2,0,1:T(8,128)}, u32[]{:S(2)}, u32[]{:S(2)}) collective-permute-start(f32[128,4,128]{2,0,1:T(8,128)S(1)} %get-tuple-element.1613), channel_id=1, source_target_pairs={{0,2},{2,4},{4,6},{6,8},{8,10},{10,12},{12,14},{14,16},{16,18},{18... | collective-permute-start | bytes 786440 | tf_op jit(solution)/shard_map/while/body/eval_jaxpr/ppermute | solution.py:14
  1109.8 6.6 collective-permute-done.2
  1128.1 8.3 conditional.32
  1136.4 23.7 %collective-permute-start.3 = (f32[128,4,128]{2,0,1:T(8,128)}, f32[128,4,128]{2,0,1:T(8,128)}, u32[]{:S(2)}, u32[]{:S(2)}) collective-permute-start(f32[128,4,128]{2,0,1:T(8,128)} %get-tuple-element.1612), channel_id=1, source_target_pairs={{0,2},{2,4},{4,6},{6,8},{8,10},{10,12},{12,14},{14,16},{16,18},{18... | collective-permute-start | bytes 786440 | tf_op jit(solution)/shard_map/while/body/eval_jaxpr/ppermute | solution.py:14
  1160.1 9.1 collective-permute-start.4
  1198.4 8.3 conditional.32
  1206.7 9.6 conditional.33
  1220.1 26.1 %collective-permute-start.4 = (f32[128,4,128]{2,0,1:T(8,128)S(1)}, f32[128,4,128]{2,0,1:T(8,128)}, u32[]{:S(2)}, u32[]{:S(2)}) collective-permute-start(f32[128,4,128]{2,0,1:T(8,128)S(1)} %get-tuple-element.1613), channel_id=1, source_target_pairs={{0,2},{2,4},{4,6},{6,8},{8,10},{10,12},{12,14},{14,16},{16,18},{18... | collective-permute-start | bytes 786440 | tf_op jit(solution)/shard_map/while/body/eval_jaxpr/ppermute | solution.py:14
  1272.4 9.6 conditional.33
  1284.8 18.4 %collective-permute-start.4 = (f32[128,4,128]{2,0,1:T(8,128)S(1)}, f32[128,4,128]{2,0,1:T(8,128)}, u32[]{:S(2)}, u32[]{:S(2)}) collective-permute-start(f32[128,4,128]{2,0,1:T(8,128)S(1)} %get-tuple-element.1613), channel_id=1, source_target_pairs={{0,2},{2,4},{4,6},{6,8},{8,10},{10,12},{12,14},{14,16},{16,18},{18... | collective-permute-start | bytes 786440 | tf_op jit(solution)/shard_map/while/body/eval_jaxpr/ppermute | solution.py:14
  1303.1 10.8 collective-permute-start.1
  1318.6 7.3 collective-permute-done.2
  1339.5 38.9 %collective-permute-start.4 = (f32[128,4,128]{2,0,1:T(8,128)S(1)}, f32[128,4,128]{2,0,1:T(8,128)}, u32[]{:S(2)}, u32[]{:S(2)}) collective-permute-start(f32[128,4,128]{2,0,1:T(8,128)S(1)} %get-tuple-element.1613), channel_id=1, source_target_pairs={{0,2},{2,4},{4,6},{6,8},{8,10},{10,12},{12,14},{14,16},{16,18},{18... | collective-permute-start | bytes 786440 | tf_op jit(solution)/shard_map/while/body/eval_jaxpr/ppermute | solution.py:14
  1380.3 13.7 collective-permute-start.2
  1409.6 8.3 conditional.32
  1417.9 9.6 conditional.33
  1429.5 22.3 %collective-permute-start.4 = (f32[128,4,128]{2,0,1:T(8,128)S(1)}, f32[128,4,128]{2,0,1:T(8,128)}, u32[]{:S(2)}, u32[]{:S(2)}) collective-permute-start(f32[128,4,128]{2,0,1:T(8,128)S(1)} %get-tuple-element.1613), channel_id=1, source_target_pairs={{0,2},{2,4},{4,6},{6,8},{8,10},{10,12},{12,14},{14,16},{16,18},{18... | collective-permute-start | bytes 786440 | tf_op jit(solution)/shard_map/while/body/eval_jaxpr/ppermute | solution.py:14
  1451.8 7.6 collective-permute-start.1
  1464.0 7.2 collective-permute-done.2
  1480.3 12.7 collective-permute-done.5
  (1201 shorter events, 887.6 us)
Async XLA Ops:
  29.9 15.3 %collective-permute-start = (bf16[128,4,128]{2,0,1:T(8,128)(2,1)S(1)}, bf16[128,4,128]{2,0,1:T(8,128)(2,1)S(1)}, u32[]{:S(2)}, u32[]{:S(2)}) collective-permute-start(bf16[128,4,128]{2,0,1:T(8,128)(2,1)S(1)} %get-tuple-element.1673), channel_id=1, source_target_pairs={{0,2},{2,4},{4,6},{6,8},{8,10},{10,12},{12,14},{14,16},{16,18},{18... | collective-permute-start | bytes 393224 | tf_op jit(solution)/shard_map/while/body/eval_jaxpr/ppermute | solution.py:14
  51.8 12.3 collective-permute-start
  70.7 12.7 collective-permute-start
  138.2 12.4 collective-permute-start
  175.6 14.5 collective-permute-start
  229.7 15.1 %collective-permute-start = (bf16[128,4,128]{2,0,1:T(8,128)(2,1)S(1)}, bf16[128,4,128]{2,0,1:T(8,128)(2,1)S(1)}, u32[]{:S(2)}, u32[]{:S(2)}) collective-permute-start(bf16[128,4,128]{2,0,1:T(8,128)(2,1)S(1)} %get-tuple-element.1673), channel_id=1, source_target_pairs={{0,2},{2,4},{4,6},{6,8},{8,10},{10,12},{12,14},{14,16},{16,18},{18... | collective-permute-start | bytes 393224 | tf_op jit(solution)/shard_map/while/body/eval_jaxpr/ppermute | solution.py:14
  251.4 13.7 collective-permute-start
  268.8 12.9 collective-permute-start
  341.0 23.9 %collective-permute-start.3 = (f32[128,4,128]{2,0,1:T(8,128)}, f32[128,4,128]{2,0,1:T(8,128)}, u32[]{:S(2)}, u32[]{:S(2)}) collective-permute-start(f32[128,4,128]{2,0,1:T(8,128)} %get-tuple-element.1612), channel_id=1, source_target_pairs={{0,2},{2,4},{4,6},{6,8},{8,10},{10,12},{12,14},{14,16},{16,18},{18... | collective-permute-start | bytes 786440 | tf_op jit(solution)/shard_map/while/body/eval_jaxpr/ppermute | solution.py:14
  347.4 19.2 %collective-permute-start.4 = (f32[128,4,128]{2,0,1:T(8,128)S(1)}, f32[128,4,128]{2,0,1:T(8,128)}, u32[]{:S(2)}, u32[]{:S(2)}) collective-permute-start(f32[128,4,128]{2,0,1:T(8,128)S(1)} %get-tuple-element.1613), channel_id=1, source_target_pairs={{0,2},{2,4},{4,6},{6,8},{8,10},{10,12},{12,14},{14,16},{16,18},{18... | collective-permute-start | bytes 786440 | tf_op jit(solution)/shard_map/while/body/eval_jaxpr/ppermute | solution.py:14
  403.4 32.2 %collective-permute-start.3 = (f32[128,4,128]{2,0,1:T(8,128)}, f32[128,4,128]{2,0,1:T(8,128)}, u32[]{:S(2)}, u32[]{:S(2)}) collective-permute-start(f32[128,4,128]{2,0,1:T(8,128)} %get-tuple-element.1612), channel_id=1, source_target_pairs={{0,2},{2,4},{4,6},{6,8},{8,10},{10,12},{12,14},{14,16},{16,18},{18... | collective-permute-start | bytes 786440 | tf_op jit(solution)/shard_map/while/body/eval_jaxpr/ppermute | solution.py:14
  409.1 28.1 %collective-permute-start.4 = (f32[128,4,128]{2,0,1:T(8,128)S(1)}, f32[128,4,128]{2,0,1:T(8,128)}, u32[]{:S(2)}, u32[]{:S(2)}) collective-permute-start(f32[128,4,128]{2,0,1:T(8,128)S(1)} %get-tuple-element.1613), channel_id=1, source_target_pairs={{0,2},{2,4},{4,6},{6,8},{8,10},{10,12},{12,14},{14,16},{16,18},{18... | collective-permute-start | bytes 786440 | tf_op jit(solution)/shard_map/while/body/eval_jaxpr/ppermute | solution.py:14
  431.7 12.1 collective-permute-start.1
  475.1 32.0 %collective-permute-start.3 = (f32[128,4,128]{2,0,1:T(8,128)}, f32[128,4,128]{2,0,1:T(8,128)}, u32[]{:S(2)}, u32[]{:S(2)}) collective-permute-start(f32[128,4,128]{2,0,1:T(8,128)} %get-tuple-element.1612), channel_id=1, source_target_pairs={{0,2},{2,4},{4,6},{6,8},{8,10},{10,12},{12,14},{14,16},{16,18},{18... | collective-permute-start | bytes 786440 | tf_op jit(solution)/shard_map/while/body/eval_jaxpr/ppermute | solution.py:14
  498.3 14.6 collective-permute-start.4
  500.8 14.6 collective-permute-start.1
  505.2 13.1 collective-permute-start.2
  547.9 36.5 %collective-permute-start.3 = (f32[128,4,128]{2,0,1:T(8,128)}, f32[128,4,128]{2,0,1:T(8,128)}, u32[]{:S(2)}, u32[]{:S(2)}) collective-permute-start(f32[128,4,128]{2,0,1:T(8,128)} %get-tuple-element.1612), channel_id=1, source_target_pairs={{0,2},{2,4},{4,6},{6,8},{8,10},{10,12},{12,14},{14,16},{16,18},{18... | collective-permute-start | bytes 786440 | tf_op jit(solution)/shard_map/while/body/eval_jaxpr/ppermute | solution.py:14
  572.3 17.0 %collective-permute-start.4 = (f32[128,4,128]{2,0,1:T(8,128)S(1)}, f32[128,4,128]{2,0,1:T(8,128)}, u32[]{:S(2)}, u32[]{:S(2)}) collective-permute-start(f32[128,4,128]{2,0,1:T(8,128)S(1)} %get-tuple-element.1613), channel_id=1, source_target_pairs={{0,2},{2,4},{4,6},{6,8},{8,10},{10,12},{12,14},{14,16},{16,18},{18... | collective-permute-start | bytes 786440 | tf_op jit(solution)/shard_map/while/body/eval_jaxpr/ppermute | solution.py:14
  574.2 17.7 %collective-permute-start.1 = (bf16[128,4,128]{2,0,1:T(8,128)(2,1)}, bf16[128,4,128]{2,0,1:T(8,128)(2,1)}, u32[]{:S(2)}, u32[]{:S(2)}) collective-permute-start(bf16[128,4,128]{2,0,1:T(8,128)(2,1)} %copy.184), channel_id=1, source_target_pairs={{0,2},{2,4},{4,6},{6,8},{8,10},{10,12},{12,14},{14,16},{16,18},{18... | collective-permute-start | bytes 393224 | tf_op jit(solution)/shard_map/while/body/eval_jaxpr/ppermute | solution.py:14
  576.2 17.3 %collective-permute-start.2 = (bf16[128,4,128]{2,0,1:T(8,128)(2,1)S(1)}, bf16[128,4,128]{2,0,1:T(8,128)(2,1)}, u32[]{:S(2)}, u32[]{:S(2)}) collective-permute-start(bf16[128,4,128]{2,0,1:T(8,128)(2,1)S(1)} %copy.185), channel_id=1, source_target_pairs={{0,2},{2,4},{4,6},{6,8},{8,10},{10,12},{12,14},{14,16},{16,18},{18... | collective-permute-start | bytes 393224 | tf_op jit(solution)/shard_map/while/body/eval_jaxpr/ppermute | solution.py:14
  623.1 27.4 %collective-permute-start.3 = (f32[128,4,128]{2,0,1:T(8,128)}, f32[128,4,128]{2,0,1:T(8,128)}, u32[]{:S(2)}, u32[]{:S(2)}) collective-permute-start(f32[128,4,128]{2,0,1:T(8,128)} %get-tuple-element.1612), channel_id=1, source_target_pairs={{0,2},{2,4},{4,6},{6,8},{8,10},{10,12},{12,14},{14,16},{16,18},{18... | collective-permute-start | bytes 786440 | tf_op jit(solution)/shard_map/while/body/eval_jaxpr/ppermute | solution.py:14
  628.1 29.0 %collective-permute-start.4 = (f32[128,4,128]{2,0,1:T(8,128)S(1)}, f32[128,4,128]{2,0,1:T(8,128)}, u32[]{:S(2)}, u32[]{:S(2)}) collective-permute-start(f32[128,4,128]{2,0,1:T(8,128)S(1)} %get-tuple-element.1613), channel_id=1, source_target_pairs={{0,2},{2,4},{4,6},{6,8},{8,10},{10,12},{12,14},{14,16},{16,18},{18... | collective-permute-start | bytes 786440 | tf_op jit(solution)/shard_map/while/body/eval_jaxpr/ppermute | solution.py:14
  646.6 14.7 collective-permute-start.1
  648.5 14.5 collective-permute-start.2
  684.3 41.8 %collective-permute-start.3 = (f32[128,4,128]{2,0,1:T(8,128)}, f32[128,4,128]{2,0,1:T(8,128)}, u32[]{:S(2)}, u32[]{:S(2)}) collective-permute-start(f32[128,4,128]{2,0,1:T(8,128)} %get-tuple-element.1612), channel_id=1, source_target_pairs={{0,2},{2,4},{4,6},{6,8},{8,10},{10,12},{12,14},{14,16},{16,18},{18... | collective-permute-start | bytes 786440 | tf_op jit(solution)/shard_map/while/body/eval_jaxpr/ppermute | solution.py:14
  698.9 28.9 %collective-permute-start.4 = (f32[128,4,128]{2,0,1:T(8,128)S(1)}, f32[128,4,128]{2,0,1:T(8,128)}, u32[]{:S(2)}, u32[]{:S(2)}) collective-permute-start(f32[128,4,128]{2,0,1:T(8,128)S(1)} %get-tuple-element.1613), channel_id=1, source_target_pairs={{0,2},{2,4},{4,6},{6,8},{8,10},{10,12},{12,14},{14,16},{16,18},{18... | collective-permute-start | bytes 786440 | tf_op jit(solution)/shard_map/while/body/eval_jaxpr/ppermute | solution.py:14
  724.2 12.8 collective-permute-start.2
  757.0 41.8 %collective-permute-start.3 = (f32[128,4,128]{2,0,1:T(8,128)}, f32[128,4,128]{2,0,1:T(8,128)}, u32[]{:S(2)}, u32[]{:S(2)}) collective-permute-start(f32[128,4,128]{2,0,1:T(8,128)} %get-tuple-element.1612), channel_id=1, source_target_pairs={{0,2},{2,4},{4,6},{6,8},{8,10},{10,12},{12,14},{14,16},{16,18},{18... | collective-permute-start | bytes 786440 | tf_op jit(solution)/shard_map/while/body/eval_jaxpr/ppermute | solution.py:14
  763.9 36.6 %collective-permute-start.4 = (f32[128,4,128]{2,0,1:T(8,128)S(1)}, f32[128,4,128]{2,0,1:T(8,128)}, u32[]{:S(2)}, u32[]{:S(2)}) collective-permute-start(f32[128,4,128]{2,0,1:T(8,128)S(1)} %get-tuple-element.1613), channel_id=1, source_target_pairs={{0,2},{2,4},{4,6},{6,8},{8,10},{10,12},{12,14},{14,16},{16,18},{18... | collective-permute-start | bytes 786440 | tf_op jit(solution)/shard_map/while/body/eval_jaxpr/ppermute | solution.py:14
  791.2 15.6 %collective-permute-start.1 = (bf16[128,4,128]{2,0,1:T(8,128)(2,1)}, bf16[128,4,128]{2,0,1:T(8,128)(2,1)}, u32[]{:S(2)}, u32[]{:S(2)}) collective-permute-start(bf16[128,4,128]{2,0,1:T(8,128)(2,1)} %copy.184), channel_id=1, source_target_pairs={{0,2},{2,4},{4,6},{6,8},{8,10},{10,12},{12,14},{14,16},{16,18},{18... | collective-permute-start | bytes 393224 | tf_op jit(solution)/shard_map/while/body/eval_jaxpr/ppermute | solution.py:14
  796.9 17.7 %collective-permute-start.2 = (bf16[128,4,128]{2,0,1:T(8,128)(2,1)S(1)}, bf16[128,4,128]{2,0,1:T(8,128)(2,1)}, u32[]{:S(2)}, u32[]{:S(2)}) collective-permute-start(bf16[128,4,128]{2,0,1:T(8,128)(2,1)S(1)} %copy.185), channel_id=1, source_target_pairs={{0,2},{2,4},{4,6},{6,8},{8,10},{10,12},{12,14},{14,16},{16,18},{18... | collective-permute-start | bytes 393224 | tf_op jit(solution)/shard_map/while/body/eval_jaxpr/ppermute | solution.py:14
  844.3 33.8 %collective-permute-start.3 = (f32[128,4,128]{2,0,1:T(8,128)}, f32[128,4,128]{2,0,1:T(8,128)}, u32[]{:S(2)}, u32[]{:S(2)}) collective-permute-start(f32[128,4,128]{2,0,1:T(8,128)} %get-tuple-element.1612), channel_id=1, source_target_pairs={{0,2},{2,4},{4,6},{6,8},{8,10},{10,12},{12,14},{14,16},{16,18},{18... | collective-permute-start | bytes 786440 | tf_op jit(solution)/shard_map/while/body/eval_jaxpr/ppermute | solution.py:14
  848.1 32.5 %collective-permute-start.4 = (f32[128,4,128]{2,0,1:T(8,128)S(1)}, f32[128,4,128]{2,0,1:T(8,128)}, u32[]{:S(2)}, u32[]{:S(2)}) collective-permute-start(f32[128,4,128]{2,0,1:T(8,128)S(1)} %get-tuple-element.1613), channel_id=1, source_target_pairs={{0,2},{2,4},{4,6},{6,8},{8,10},{10,12},{12,14},{14,16},{16,18},{18... | collective-permute-start | bytes 786440 | tf_op jit(solution)/shard_map/while/body/eval_jaxpr/ppermute | solution.py:14
  868.3 19.0 %collective-permute-start.1 = (bf16[128,4,128]{2,0,1:T(8,128)(2,1)}, bf16[128,4,128]{2,0,1:T(8,128)(2,1)}, u32[]{:S(2)}, u32[]{:S(2)}) collective-permute-start(bf16[128,4,128]{2,0,1:T(8,128)(2,1)} %copy.184), channel_id=1, source_target_pairs={{0,2},{2,4},{4,6},{6,8},{8,10},{10,12},{12,14},{14,16},{16,18},{18... | collective-permute-start | bytes 393224 | tf_op jit(solution)/shard_map/while/body/eval_jaxpr/ppermute | solution.py:14
  876.1 14.4 collective-permute-start.2
  920.2 30.6 %collective-permute-start.3 = (f32[128,4,128]{2,0,1:T(8,128)}, f32[128,4,128]{2,0,1:T(8,128)}, u32[]{:S(2)}, u32[]{:S(2)}) collective-permute-start(f32[128,4,128]{2,0,1:T(8,128)} %get-tuple-element.1612), channel_id=1, source_target_pairs={{0,2},{2,4},{4,6},{6,8},{8,10},{10,12},{12,14},{14,16},{16,18},{18... | collective-permute-start | bytes 786440 | tf_op jit(solution)/shard_map/while/body/eval_jaxpr/ppermute | solution.py:14
  935.8 16.7 %collective-permute-start.4 = (f32[128,4,128]{2,0,1:T(8,128)S(1)}, f32[128,4,128]{2,0,1:T(8,128)}, u32[]{:S(2)}, u32[]{:S(2)}) collective-permute-start(f32[128,4,128]{2,0,1:T(8,128)S(1)} %get-tuple-element.1613), channel_id=1, source_target_pairs={{0,2},{2,4},{4,6},{6,8},{8,10},{10,12},{12,14},{14,16},{16,18},{18... | collective-permute-start | bytes 786440 | tf_op jit(solution)/shard_map/while/body/eval_jaxpr/ppermute | solution.py:14
  943.0 14.7 collective-permute-start.1
  948.8 12.6 collective-permute-start.2
  991.0 33.8 %collective-permute-start.3 = (f32[128,4,128]{2,0,1:T(8,128)}, f32[128,4,128]{2,0,1:T(8,128)}, u32[]{:S(2)}, u32[]{:S(2)}) collective-permute-start(f32[128,4,128]{2,0,1:T(8,128)} %get-tuple-element.1612), channel_id=1, source_target_pairs={{0,2},{2,4},{4,6},{6,8},{8,10},{10,12},{12,14},{14,16},{16,18},{18... | collective-permute-start | bytes 786440 | tf_op jit(solution)/shard_map/while/body/eval_jaxpr/ppermute | solution.py:14
  1004.8 24.1 %collective-permute-start.4 = (f32[128,4,128]{2,0,1:T(8,128)S(1)}, f32[128,4,128]{2,0,1:T(8,128)}, u32[]{:S(2)}, u32[]{:S(2)}) collective-permute-start(f32[128,4,128]{2,0,1:T(8,128)S(1)} %get-tuple-element.1613), channel_id=1, source_target_pairs={{0,2},{2,4},{4,6},{6,8},{8,10},{10,12},{12,14},{14,16},{16,18},{18... | collective-permute-start | bytes 786440 | tf_op jit(solution)/shard_map/while/body/eval_jaxpr/ppermute | solution.py:14
  1064.6 39.2 %collective-permute-start.3 = (f32[128,4,128]{2,0,1:T(8,128)}, f32[128,4,128]{2,0,1:T(8,128)}, u32[]{:S(2)}, u32[]{:S(2)}) collective-permute-start(f32[128,4,128]{2,0,1:T(8,128)} %get-tuple-element.1612), channel_id=1, source_target_pairs={{0,2},{2,4},{4,6},{6,8},{8,10},{10,12},{12,14},{14,16},{16,18},{18... | collective-permute-start | bytes 786440 | tf_op jit(solution)/shard_map/while/body/eval_jaxpr/ppermute | solution.py:14
  1066.5 39.0 %collective-permute-start.4 = (f32[128,4,128]{2,0,1:T(8,128)S(1)}, f32[128,4,128]{2,0,1:T(8,128)}, u32[]{:S(2)}, u32[]{:S(2)}) collective-permute-start(f32[128,4,128]{2,0,1:T(8,128)S(1)} %get-tuple-element.1613), channel_id=1, source_target_pairs={{0,2},{2,4},{4,6},{6,8},{8,10},{10,12},{12,14},{14,16},{16,18},{18... | collective-permute-start | bytes 786440 | tf_op jit(solution)/shard_map/while/body/eval_jaxpr/ppermute | solution.py:14
  1096.8 13.0 collective-permute-start.1
  1101.8 14.6 collective-permute-start.2
  1136.4 40.3 %collective-permute-start.3 = (f32[128,4,128]{2,0,1:T(8,128)}, f32[128,4,128]{2,0,1:T(8,128)}, u32[]{:S(2)}, u32[]{:S(2)}) collective-permute-start(f32[128,4,128]{2,0,1:T(8,128)} %get-tuple-element.1612), channel_id=1, source_target_pairs={{0,2},{2,4},{4,6},{6,8},{8,10},{10,12},{12,14},{14,16},{16,18},{18... | collective-permute-start | bytes 786440 | tf_op jit(solution)/shard_map/while/body/eval_jaxpr/ppermute | solution.py:14
  1160.1 18.3 %collective-permute-start.4 = (f32[128,4,128]{2,0,1:T(8,128)S(1)}, f32[128,4,128]{2,0,1:T(8,128)}, u32[]{:S(2)}, u32[]{:S(2)}) collective-permute-start(f32[128,4,128]{2,0,1:T(8,128)S(1)} %get-tuple-element.1613), channel_id=1, source_target_pairs={{0,2},{2,4},{4,6},{6,8},{8,10},{10,12},{12,14},{14,16},{16,18},{18... | collective-permute-start | bytes 786440 | tf_op jit(solution)/shard_map/while/body/eval_jaxpr/ppermute | solution.py:14
  1169.2 13.4 collective-permute-start.1
  1216.4 33.7 %collective-permute-start.3 = (f32[128,4,128]{2,0,1:T(8,128)}, f32[128,4,128]{2,0,1:T(8,128)}, u32[]{:S(2)}, u32[]{:S(2)}) collective-permute-start(f32[128,4,128]{2,0,1:T(8,128)} %get-tuple-element.1612), channel_id=1, source_target_pairs={{0,2},{2,4},{4,6},{6,8},{8,10},{10,12},{12,14},{14,16},{16,18},{18... | collective-permute-start | bytes 786440 | tf_op jit(solution)/shard_map/while/body/eval_jaxpr/ppermute | solution.py:14
  1220.1 32.5 %collective-permute-start.4 = (f32[128,4,128]{2,0,1:T(8,128)S(1)}, f32[128,4,128]{2,0,1:T(8,128)}, u32[]{:S(2)}, u32[]{:S(2)}) collective-permute-start(f32[128,4,128]{2,0,1:T(8,128)S(1)} %get-tuple-element.1613), channel_id=1, source_target_pairs={{0,2},{2,4},{4,6},{6,8},{8,10},{10,12},{12,14},{14,16},{16,18},{18... | collective-permute-start | bytes 786440 | tf_op jit(solution)/shard_map/while/body/eval_jaxpr/ppermute | solution.py:14
  1246.2 13.0 collective-permute-start.1
  1248.1 12.5 collective-permute-start.2
  1282.0 33.9 %collective-permute-start.3 = (f32[128,4,128]{2,0,1:T(8,128)}, f32[128,4,128]{2,0,1:T(8,128)}, u32[]{:S(2)}, u32[]{:S(2)}) collective-permute-start(f32[128,4,128]{2,0,1:T(8,128)} %get-tuple-element.1612), channel_id=1, source_target_pairs={{0,2},{2,4},{4,6},{6,8},{8,10},{10,12},{12,14},{14,16},{16,18},{18... | collective-permute-start | bytes 786440 | tf_op jit(solution)/shard_map/while/body/eval_jaxpr/ppermute | solution.py:14
  1284.8 32.8 %collective-permute-start.4 = (f32[128,4,128]{2,0,1:T(8,128)S(1)}, f32[128,4,128]{2,0,1:T(8,128)}, u32[]{:S(2)}, u32[]{:S(2)}) collective-permute-start(f32[128,4,128]{2,0,1:T(8,128)S(1)} %get-tuple-element.1613), channel_id=1, source_target_pairs={{0,2},{2,4},{4,6},{6,8},{8,10},{10,12},{12,14},{14,16},{16,18},{18... | collective-permute-start | bytes 786440 | tf_op jit(solution)/shard_map/while/body/eval_jaxpr/ppermute | solution.py:14
  1303.1 15.4 %collective-permute-start.1 = (bf16[128,4,128]{2,0,1:T(8,128)(2,1)}, bf16[128,4,128]{2,0,1:T(8,128)(2,1)}, u32[]{:S(2)}, u32[]{:S(2)}) collective-permute-start(bf16[128,4,128]{2,0,1:T(8,128)(2,1)} %copy.184), channel_id=1, source_target_pairs={{0,2},{2,4},{4,6},{6,8},{8,10},{10,12},{12,14},{14,16},{16,18},{18... | collective-permute-start | bytes 393224 | tf_op jit(solution)/shard_map/while/body/eval_jaxpr/ppermute | solution.py:14
  1337.6 56.4 %collective-permute-start.3 = (f32[128,4,128]{2,0,1:T(8,128)}, f32[128,4,128]{2,0,1:T(8,128)}, u32[]{:S(2)}, u32[]{:S(2)}) collective-permute-start(f32[128,4,128]{2,0,1:T(8,128)} %get-tuple-element.1612), channel_id=1, source_target_pairs={{0,2},{2,4},{4,6},{6,8},{8,10},{10,12},{12,14},{14,16},{16,18},{18... | collective-permute-start | bytes 786440 | tf_op jit(solution)/shard_map/while/body/eval_jaxpr/ppermute | solution.py:14
  1339.5 56.2 %collective-permute-start.4 = (f32[128,4,128]{2,0,1:T(8,128)S(1)}, f32[128,4,128]{2,0,1:T(8,128)}, u32[]{:S(2)}, u32[]{:S(2)}) collective-permute-start(f32[128,4,128]{2,0,1:T(8,128)S(1)} %get-tuple-element.1613), channel_id=1, source_target_pairs={{0,2},{2,4},{4,6},{6,8},{8,10},{10,12},{12,14},{14,16},{16,18},{18... | collective-permute-start | bytes 786440 | tf_op jit(solution)/shard_map/while/body/eval_jaxpr/ppermute | solution.py:14
  1378.3 18.3 %collective-permute-start.1 = (bf16[128,4,128]{2,0,1:T(8,128)(2,1)}, bf16[128,4,128]{2,0,1:T(8,128)(2,1)}, u32[]{:S(2)}, u32[]{:S(2)}) collective-permute-start(bf16[128,4,128]{2,0,1:T(8,128)(2,1)} %copy.184), channel_id=1, source_target_pairs={{0,2},{2,4},{4,6},{6,8},{8,10},{10,12},{12,14},{14,16},{16,18},{18... | collective-permute-start | bytes 393224 | tf_op jit(solution)/shard_map/while/body/eval_jaxpr/ppermute | solution.py:14
  1380.3 17.6 %collective-permute-start.2 = (bf16[128,4,128]{2,0,1:T(8,128)(2,1)S(1)}, bf16[128,4,128]{2,0,1:T(8,128)(2,1)}, u32[]{:S(2)}, u32[]{:S(2)}) collective-permute-start(bf16[128,4,128]{2,0,1:T(8,128)(2,1)S(1)} %copy.185), channel_id=1, source_target_pairs={{0,2},{2,4},{4,6},{6,8},{8,10},{10,12},{12,14},{14,16},{16,18},{18... | collective-permute-start | bytes 393224 | tf_op jit(solution)/shard_map/while/body/eval_jaxpr/ppermute | solution.py:14
  1427.5 33.8 %collective-permute-start.3 = (f32[128,4,128]{2,0,1:T(8,128)}, f32[128,4,128]{2,0,1:T(8,128)}, u32[]{:S(2)}, u32[]{:S(2)}) collective-permute-start(f32[128,4,128]{2,0,1:T(8,128)} %get-tuple-element.1612), channel_id=1, source_target_pairs={{0,2},{2,4},{4,6},{6,8},{8,10},{10,12},{12,14},{14,16},{16,18},{18... | collective-permute-start | bytes 786440 | tf_op jit(solution)/shard_map/while/body/eval_jaxpr/ppermute | solution.py:14
  1429.5 33.5 %collective-permute-start.4 = (f32[128,4,128]{2,0,1:T(8,128)S(1)}, f32[128,4,128]{2,0,1:T(8,128)}, u32[]{:S(2)}, u32[]{:S(2)}) collective-permute-start(f32[128,4,128]{2,0,1:T(8,128)S(1)} %get-tuple-element.1613), channel_id=1, source_target_pairs={{0,2},{2,4},{4,6},{6,8},{8,10},{10,12},{12,14},{14,16},{16,18},{18... | collective-permute-start | bytes 786440 | tf_op jit(solution)/shard_map/while/body/eval_jaxpr/ppermute | solution.py:14
  1451.8 12.2 collective-permute-start.1
  1476.3 16.7 %collective-permute-start.5 = (bf16[1,128,32,128]{3,2,1,0:T(8,128)(2,1)S(1)}, bf16[1,128,32,128]{3,2,1,0:T(8,128)(2,1)S(1)}, u32[]{:S(2)}, u32[]{:S(2)}) collective-permute-start(bf16[1,128,32,128]{3,2,1,0:T(8,128)(2,1)S(1)} %bitcast.340), channel_id=1, source_target_pairs={{32,0},{64,32},{96,64},{128,96},{160,128},{192,160},{224,192},{256... | collective-permute-start | bytes 3145736 | tf_op jit(solution)/shard_map/ppermute | solution.py:20
  (135 other events, 563.7 us)
where the time goes:
time: 1520 us; the launch traced here: 1490 us
  starting transfers between devices  649 us (43%)
  local copies, waits for them, and re-layouts  248 us (16%)
  waiting for transfers between devices  174 us (11%)
  matrix products  167 us (11%)
  loops' own time  153 us (10%)
  other arithmetic  97.3 us (6%)
    ppermute x79, starting transfers between devices, passed_along(): return lax.ppermute(value, axis, pairs)  647 us
    ppermute x79, waiting for transfers between devices, passed_along(): return lax.ppermute(value, axis, pairs)  162 us
    while x111, local copies, waits for them, and re-layouts  81.7 us
    another operation x1, loops' own time, shards(): lax.fori_loop(0, cycle_size, cycle_step, (dq_init, (k_rot, v_heads), (acc...  76.8 us
    dot_general x27, matrix products, pair_grads(): jnp.einsum('agij,jad->iagd', dscore, k_rows, preferred_element_type=jnp.f...  72.6 us
    another operation x1, loops' own time, shards(): lax.fori_loop(1, cycle_size, stat_step, (row_stats, k_rot))  48.6 us
    dot_general x27, matrix products, pair_grads(): jnp.einsum('iagd,jad->agij', q_rows, k_rows, preferred_element_type=jnp.f...  39.9 us
  transfers between devices with their start and end apart: 80, of which 48 were waited for; matrix products, arithmetic and copies ran while one was open for 5% of the time, Pallas kernels for 0%

commit v1 on v0

v1 whole, which is shorter than its diff:
```python
import math

import jax
import jax.numpy as jnp
import numpy as np
from jax import lax
from jax.experimental import pallas as pl
from jax.experimental.pallas import tpu as pltpu
from jax.sharding import PartitionSpec as P

MESH = pl.DeviceIdType.MESH
NEG = -1e30
F32 = jnp.float32
BF16 = jnp.bfloat16
NY = 8
LOOK = 2
CHUNK = 256


def signs(size):
    index = np.arange(size)
    ands = index[:, None] & index[None, :]
    parity = np.zeros((size, size), np.int64)
    for bit in range(size.bit_length() - 1):
        parity ^= (ands >> bit) & 1
    return 1.0 - 2.0 * parity


def dot(a, b):
    return jnp.dot(a, b, preferred_element_type=F32)


def split3(x):
    a = x.astype(BF16)
    r = x - a.astype(F32)
    b = r.astype(BF16)
    c = (r - b.astype(F32)).astype(BF16)
    return a, b, c


def kernel(
    bo, kv_in, had, q_hbm, g_hbm, o_hbm,
    kg, vg, hand,
    q_v, g_v, o_v, kv, qr, qt, gr, gt, delta, qpos, m8, l8, lse, scores, ds_buf, pl_buf, dqt,
    rs_out, rs_in, total, fin, hs, zero_buf,
    loc_sem, ag_send, ag_recv, rs_send, rs_recv, h_send, h_recv,
):
    head_size = 128
    inv = np.float32(1.0 / math.sqrt(head_size))
    to_log2 = np.float32(math.log2(math.e) / math.sqrt(head_size))
    pipe = lax.axis_index("pipe")
    ctx = lax.axis_index("ctx")
    head = lax.axis_index("head")
    n_pipe = lax.axis_size("pipe")
    y = ctx // 2
    zh = ctx % 2

    def ring(step):
        return (pipe, ((y + step + NY) % NY) * 2 + zh, head)

    across = (pipe, y * 2 + (1 - zh), head)
    before = ((pipe + n_pipe - 1) % n_pipe, ctx, head)
    after = ((pipe + 1) % n_pipe, ctx, head)

    barrier = pltpu.get_barrier_semaphore()
    for other in (ring(1), ring(-1), across, before, after):
        pl.semaphore_signal(barrier, inc=1, device_id=other, device_id_type=MESH)

    loads = [
        pltpu.make_async_copy(src, dst, loc_sem.at[n])
        for n, (src, dst) in enumerate(((q_hbm, q_v), (g_hbm, g_v), (o_hbm, o_v)))
    ]
    for load in loads:
        load.start()

    for g in range(4):
        kv[ctx, g, 0] = (dot(kv_in[g, 0], had[...]) * inv).astype(BF16)
        kv[ctx, g, 1] = kv_in[g, 1]

    pl.semaphore_wait(barrier, 5)

    def block_of(half, i):
        sign = (1 - 2 * (i % 2)) * (1 - 2 * half)
        y_src = (y + sign * ((i + 1) // 2) + NY) % NY
        return y_src * 2 + (zh if half == 0 else 1 - zh)

    def ag_copy(pair, half, j, src, target):
        piece = kv.at[src, pl.ds(2 * pair, 2)]
        return pltpu.make_async_remote_copy(
            src_ref=piece, dst_ref=piece,
            send_sem=ag_send.at[pair, half, j], recv_sem=ag_recv.at[pair, half, j],
            device_id=target, device_id_type=MESH,
        )

    def z_copy(pair, src):
        piece = kv.at[src, pl.ds(2 * pair, 2)]
        return pltpu.make_async_remote_copy(
            src_ref=piece, dst_ref=piece,
            send_sem=ag_send.at[pair, 0, 0], recv_sem=ag_recv.at[pair, 1, 0],
            device_id=across, device_id_type=MESH,
        )

    def ag_event(e):
        pair, i = e // NY, e % NY
        for half in range(2):
            lead = 1 - 2 * half
            src = block_of(half, i)
            if half == 1:

                @pl.when(i == 0)
                def _():
                    z_copy(pair, src).wait_recv()

            @pl.when(i > 0)
            def _():
                ag_copy(pair, half, i, src, ring(1)).wait_recv()

            @pl.when(i == 0)
            def _():
                ag_copy(pair, half, 1, src, ring(lead)).start()
                ag_copy(pair, half, 2, src, ring(-lead)).start()

            @pl.when((i > 0) & (i <= 5))
            def _():
                way = lead * (2 * (i % 2) - 1)
                ag_copy(pair, half, i + 2, src, ring(way)).start()

    for pair in range(2):
        z_copy(pair, ctx).start()

    m8[...] = jnp.full(m8.shape, NEG, F32)
    l8[...] = jnp.zeros(l8.shape, F32)
    zero_buf[...] = jnp.zeros(zero_buf.shape, BF16)
    row = lax.broadcasted_iota(jnp.int32, qpos.shape, 1)
    starts = jnp.where(row < 512, bo[2 * ctx], bo[2 * ctx + 1])
    qpos[...] = starts * 64 + ((row >> 3) & 63)

    def prep(j, _):
        toks = pl.ds(pl.multiple_of(j * 16, 16), 16)
        rows = pl.ds(pl.multiple_of(j * 128, 128), 128)
        q_c = q_v[toks].astype(F32)
        g_c = g_v[toks].astype(F32)
        o_c = o_v[toks].astype(F32)
        for g in range(4):
            hd = slice(8 * g, 8 * g + 8)
            q_g = q_c[:, hd, :].reshape(128, 128).astype(BF16)
            rot = dot(q_g, had[...]) * inv
            qr[g, rows, :] = rot.astype(BF16)
            qt[g, :, rows] = rot.T.astype(BF16)
            g_g = g_c[:, hd, :].reshape(128, 128)
            o_g = o_c[:, hd, :].reshape(128, 128)
            gr[g, rows, :] = g_g.astype(BF16)
            gt[g, :, rows] = g_g.T.astype(BF16)
            sums = jnp.sum((g_g * o_g).T, axis=0, keepdims=True)
            delta[g, :, rows] = jnp.broadcast_to(sums, (8, 128))
        return 0

    ag_event(0)
    for load in loads:
        load.wait()
    lax.fori_loop(0, 8, prep, 0)
    lax.fori_loop(1, LOOK, lambda e, _: (ag_event(e), 0)[1], 0)

    place = (
        lax.broadcasted_iota(jnp.int32, (8, 8, CHUNK), 0) * 8
        + lax.broadcasted_iota(jnp.int32, (8, 8, CHUNK), 1)
    )

    def stat_unit(g, i):
        blocks = (block_of(0, i), block_of(1, i))
        k_two = jnp.concatenate([kv[blocks[0], g, 0], kv[blocks[1], g, 0]], axis=0)
        for c in range(1024 // CHUNK):
            cols = slice(c * CHUNK, (c + 1) * CHUNK)
            s = dot(k_two, qt[g, :, cols])
            q_at = qpos[:, cols]
            old = m8[g, :, cols]
            top = old
            parts = []
            for b in range(4):
                base = bo[2 * blocks[b // 2] + b % 2] * 64
                piece = s[64 * b : 64 * b + 64].reshape(8, 8, CHUNK) * to_log2
                piece = jnp.where(place <= (q_at - base)[None], piece, NEG)
                scores[g, blocks[b // 2], 64 * (b % 2) : 64 * (b % 2) + 64, cols] = piece.reshape(
                    64, CHUNK
                )
                top = jnp.maximum(top, jnp.max(piece, axis=0))
                parts.append(piece)
            run = l8[g, :, cols] * jnp.exp2(old - top)
            for piece in parts:
                run = run + jnp.sum(jnp.exp2(piece - top[None]), axis=0)
            m8[g, :, cols] = top
            l8[g, :, cols] = run

    def close_stats(g):
        top = jnp.max(m8[g], axis=0, keepdims=True)
        run = jnp.sum(l8[g] * jnp.exp2(m8[g] - top), axis=0, keepdims=True)
        lse[g] = jnp.broadcast_to(top + jnp.log2(run), (8, 1024))

    def rs_copy(g, j, target):
        return pltpu.make_async_remote_copy(
            src_ref=rs_out.at[g, j], dst_ref=rs_in.at[g, j],
            send_sem=rs_send.at[g, j], recv_sem=rs_recv.at[g, j],
            device_id=target, device_id_type=MESH,
        )

    def rs_z_copy(g):
        return pltpu.make_async_remote_copy(
            src_ref=rs_out.at[g, 7, :, pl.ds(0, 128)], dst_ref=rs_in.at[g, 7, :, pl.ds(0, 128)],
            send_sem=rs_send.at[g, 7], recv_sem=rs_recv.at[g, 7],
            device_id=across, device_id_type=MESH,
        )

    def hand_copy(g):
        return pltpu.make_async_remote_copy(
            src_ref=hs.at[g], dst_ref=hand.at[g],
            send_sem=h_send.at[g], recv_sem=h_recv.at[g],
            device_id=before, device_id_type=MESH,
        )

    def zero_copy(g):
        return pltpu.make_async_copy(zero_buf, hand.at[g], h_recv.at[g])

    def grad_unit(g, k, i):
        lead = 1 - 2 * k
        odd = i % 2
        sign = (2 * odd - 1) * lead
        y_dst = (y + sign * (4 - (i + 1) // 2) + NY) % NY
        first = 2 * y_dst
        k_two = jnp.concatenate([kv[first, g, 0], kv[first + 1, g, 0]], axis=0)
        v_two = jnp.concatenate([kv[first, g, 1], kv[first + 1, g, 1]], axis=0)

        @pl.when(i == 0)
        def _():
            close_stats(g)
            dqt[k] = jnp.zeros((128, 1024), F32)

        for c in range(1024 // CHUNK):
            cols = slice(c * CHUNK, (c + 1) * CHUNK)
            dp = dot(v_two, gt[g, :, cols]).reshape(2, 16, 8, CHUNK)
            s = scores[g, pl.ds(first, 2), :, cols].reshape(2, 16, 8, CHUNK)
            p = jnp.exp2(s - lse[g, :, cols][None, None])
            ds = p * (dp - delta[g, :, cols][None, None])
            ds = ds.reshape(256, CHUNK).astype(BF16)
            ds_buf[:, cols] = ds
            pl_buf[:, cols] = p.reshape(256, CHUNK).astype(BF16)
            dqt[k, :, cols] += lax.dot_general(
                k_two, ds, (((0,), (0,)), ((), ())), preferred_element_type=F32
            )
        total[0] = dot(ds_buf[...], qr[g])
        total[1] = dot(pl_buf[...], gr[g])

        @pl.when(i < 2)
        def _():
            rs_out[g, i] = total[...].astype(BF16)

        @pl.when((i >= 2) & (i < 7))
        def _():
            rs_copy(g, i - 2, ring(1)).wait_recv()
            rs_out[g, i] = (total[...] + rs_in[g, i - 2].astype(F32)).astype(BF16)

        @pl.when(i < 7)
        def _():
            rs_copy(g, i, ring(sign)).start()

        @pl.when(i == 7)
        def _():
            x = dqt[k] * inv
            a, b, c = split3(x)
            full = (dot(had[...], a) + dot(had[...], b) + dot(had[...], c)) * inv
            hs[g] = (full.T + gr[g].astype(F32)).astype(BF16)

            @pl.when(pipe > 0)
            def _():
                hand_copy(g).start()

            rs_copy(g, 5, ring(1)).wait_recv()
            rs_copy(g, 6, ring(1)).wait_recv()
            total[...] = total[...] + rs_in[g, 5].astype(F32) + rs_in[g, 6].astype(F32)
            theirs = pl.ds(pl.multiple_of((1 - zh) * 128, 128), 128)
            mine = pl.ds(pl.multiple_of(zh * 128, 128), 128)
            rs_out[g, 7, :, 0:128] = total[:, theirs].astype(BF16)
            rs_z_copy(g).start()
            fin[g] = total[:, mine]

    def finish(g):
        rs_z_copy(g).wait_recv()
        both = fin[g] + rs_in[g, 7, :, 0:128].astype(F32)
        a, b, c = split3(both[0] * inv)
        full = dot(a, had[...]) + dot(b, had[...]) + dot(c, had[...])
        kg[g] = (full * inv).astype(BF16)
        vg[g] = both[1].astype(BF16)

    def slot(t, _):
        turn, i = t // NY, t % NY

        @pl.when(t + LOOK < 2 * NY)
        def _():
            ag_event(t + LOOK)

        @pl.when(t < 2 * NY)
        def _():
            lax.fori_loop(0, 2, lambda k, _: (stat_unit(2 * turn + k, i), 0)[1], 0)

        @pl.when(t >= NY)
        def _():
            lax.fori_loop(0, 2, lambda k, _: (grad_unit(2 * turn - 2 + k, k, i), 0)[1], 0)

        return 0

    lax.fori_loop(0, 3 * NY, slot, 0)

    @pl.when(pipe == n_pipe - 1)
    def _():
        for g in range(4):
            zero_copy(g).start()

    for g in range(4):
        finish(g)

    @pl.when(pipe == n_pipe - 1)
    def _():
        for g in range(4):
            zero_copy(g).wait()

    @pl.when(pipe < n_pipe - 1)
    def _():
        for g in range(4):
            hand_copy(g).wait_recv()

    @pl.when(pipe > 0)
    def _():
        for g in range(4):
            hand_copy(g).wait_send()

    for pair in range(2):
        z_copy(pair, ctx).wait_send()
        for half in range(2):
            for j in range(1, 8):
                ag_copy(pair, half, j, ctx, ring(1)).wait_send()
    for g in range(4):
        for j in range(7):
            rs_copy(g, j, ring(1)).wait_send()
        rs_z_copy(g).wait_send()


def shards(queries, key_heads, value_heads, forward_out, output_grad, block_order):
    tok = queries.shape[1]
    kv_in = jnp.stack([key_heads[0], value_heads[0]]).transpose(2, 0, 1, 3)
    had = jnp.asarray(signs(128), BF16)
    vmem = pl.BlockSpec(memory_space=pltpu.VMEM)
    hbm = pl.BlockSpec(memory_space=pl.ANY)
    dma = pltpu.SemaphoreType.DMA
    kg, vg, hand = pl.pallas_call(
        kernel,
        out_shape=(
            jax.ShapeDtypeStruct((4, tok, 128), BF16),
            jax.ShapeDtypeStruct((4, tok, 128), BF16),
            jax.ShapeDtypeStruct((4, 8 * tok, 128), BF16),
        ),
        in_specs=[pl.BlockSpec(memory_space=pltpu.SMEM), vmem, vmem, hbm, hbm, hbm],
        out_specs=(vmem, vmem, hbm),
        scratch_shapes=[
            pltpu.VMEM((tok, 32, 128), BF16),
            pltpu.VMEM((tok, 32, 128), BF16),
            pltpu.VMEM((tok, 32, 128), BF16),
            pltpu.VMEM((16, 4, 2, 128, 128), BF16),
            pltpu.VMEM((4, 1024, 128), BF16),
            pltpu.VMEM((4, 128, 1024), BF16),
            pltpu.VMEM((4, 1024, 128), BF16),
            pltpu.VMEM((4, 128, 1024), BF16),
            pltpu.VMEM((4, 8, 1024), F32),
            pltpu.VMEM((8, 1024), jnp.int32),
            pltpu.VMEM((4, 8, 1024), F32),
            pltpu.VMEM((4, 8, 1024), F32),
            pltpu.VMEM((4, 8, 1024), F32),
            pltpu.VMEM((4, 16, 128, 1024), F32),
            pltpu.VMEM((256, 1024), BF16),
            pltpu.VMEM((256, 1024), BF16),
            pltpu.VMEM((2, 128, 1024), F32),
            pltpu.VMEM((4, 8, 2, 256, 128), BF16),
            pltpu.VMEM((4, 8, 2, 256, 128), BF16),
            pltpu.VMEM((2, 256, 128), F32),
            pltpu.VMEM((4, 2, 128, 128), F32),
            pltpu.VMEM((4, 1024, 128), BF16),
            pltpu.VMEM((1024, 128), BF16),
            dma((3,)),
            dma((2, 2, 8)),
            dma((2, 2, 8)),
            dma((4, 8)),
            dma((4, 8)),
            dma((4,)),
            dma((4,)),
        ],
        compiler_params=pltpu.CompilerParams(
            collective_id=0, has_side_effects=True, vmem_limit_bytes=60 * 1024 * 1024
        ),
        cost_estimate=pl.CostEstimate(
            flops=11_000_000_000, bytes_accessed=5_000_000, transcendentals=17_000_000
        ),
    )(block_order, kv_in, had, queries[0], output_grad[0], forward_out[0])
    key_grad = kg.transpose(1, 0, 2)[None]
    value_grad = vg.transpose(1, 0, 2)[None]
    handed = hand.reshape(4, tok, 8, 128).transpose(1, 0, 2, 3).reshape(1, tok, 32, 128)
    return (key_grad, value_grad, handed)


def solution(mesh):
    placed = P("pipe", "ctx", "head", None)
    return jax.shard_map(
        shards,
        mesh=mesh,
        in_specs=(placed,) * 5 + (P(),),
        out_specs=(placed,) * 3,
        check_vma=False,
    )
```

time: 1520 us -> 135 us (0.09)
  the two profiles are of different devices: /device:TPU:104 before, /device:TPU:134 now
where the time goes in v1:
time: 135 us; the launch traced here: 134 us
  Pallas kernels  127 us (94%)
  local copies, waits for them, and re-layouts  5.82 us (4%)
    pallas_call x1, Pallas kernels, shards(): pl.pallas_call(kernel, out_shape=(jax.ShapeDtypeStruct((4, tok, 128), BF1...  127 us
    unnamed x8, local copies, waits for them, and re-layouts  3.44 us

profile of v1, /device:TPU:134, one launch (start us, length us, event | category | flops | bytes accessed | tf_op | source)
XLA Modules:
  0.0 134.4 jit_solution(8811386262247795777)
XLA Ops:
  0.6 0.0 copy-start
  0.6 1.0 copy.10
  1.6 0.0 copy-done
  1.6 0.7 maximum_bitcast_fusion.kv_in
  2.4 127.2 %shard_map.94 = (bf16[4,128,128]{2,1,0:T(8,128)(2,1)}, bf16[4,128,128]{2,1,0:T(8,128)(2,1)}, bf16[4,1024,128]{2,1,0:T(8,128)(2,1)}) custom-call(s32[32]{0:T(128)} %bo.1, bf16[4,2,128,128]{3,2,1,0:T(8,128)(2,1)} %maximum_bitcast_fusion.kv_in, bf16[128,128]{1,0:T(8,128)(2,1)} %constant.2.clone.had, bf16[128,32,128]{2,1,0:T(8,128)(2,1)} %bitcast.20, ...), custom_call_target="tpu_custom_call" | custom-call | flops 11000000512 | bytes 5000000 | tf_op jit(solution)/shard_map/pallas_call | solution.py:353
  129.6 0.0 copy-start.1
  129.6 1.7 %copy.13 = bf16[1,128,4,128]{3,2,1,0:T(4,128)(2,1)} copy(bf16[1,128,4,128]{3,1,2,0:T(8,128)(2,1)} %bitcast.19) | data formatting | bytes 262144
  131.3 0.0 copy-done.1
  131.3 0.8 copy.14
  132.1 2.4 %copy_bitcast_fusion = bf16[1,128,32,128]{3,2,1,0:T(8,128)(2,1)} fusion(bf16[4,1024,128]{2,1,0:T(8,128)(2,1)} %get-tuple-element.8), kind=kLoop, calls=%fused_computation | loop fusion | bytes 2097152 | tf_op jit(solution)/shard_map/reshape | solution.py:403
  (1 shorter events, 0.0 us)
Async XLA Ops:
  0.6 1.0 copy-start
  129.6 1.7 %copy-start.1 = (bf16[4,128,128]{2,1,0:T(8,128)(2,1)S(1)}, bf16[4,128,128]{2,1,0:T(8,128)(2,1)}, u32[]{:S(2)}) copy-start(bf16[4,128,128]{2,1,0:T(8,128)(2,1)} %get-tuple-element.7) | copy-start | bytes 393220

commit v2 on v1

v2 whole, which is shorter than its diff:
```python
import math

import jax
import jax.numpy as jnp
import numpy as np
from jax import lax
from jax.experimental import pallas as pl
from jax.experimental.pallas import tpu as pltpu
from jax.sharding import PartitionSpec as P

MESH = pl.DeviceIdType.MESH
NEG = -1e30
F32 = jnp.float32
BF16 = jnp.bfloat16
NY = 8
ROWS_AT = 4
REST = 8 - 2 * (NY - ROWS_AT - 2)
LAG = 2
AHEAD = LAG + 2
Z_STEPS = (None, None, 3)
CHUNK = 512


def signs(size):
    index = np.arange(size)
    ands = index[:, None] & index[None, :]
    parity = np.zeros((size, size), np.int64)
    for bit in range(size.bit_length() - 1):
        parity ^= (ands >> bit) & 1
    return 1.0 - 2.0 * parity


def dot(a, b):
    return jnp.dot(a, b, preferred_element_type=F32)


def split3(x):
    a = x.astype(BF16)
    r = x - a.astype(F32)
    b = r.astype(BF16)
    c = (r - b.astype(F32)).astype(BF16)
    return a, b, c


def kernel(
    bo, kv_in, had, q_hbm, g_hbm, o_hbm,
    kg, vg, hand,
    q_v, g_v, o_v, kv, qr, qt, gr, gt, delta, qpos, m8, l8, lse, scores, ds_buf, pl_buf, dqt,
    rs_out, rs_in, part, total, fin, hs, zero_buf,
    loc_sem, row_send, row_recv, ag_send, ag_recv, rs_send, rs_recv, h_send, h_recv,
):
    head_size = 128
    inv = np.float32(1.0 / math.sqrt(head_size))
    to_log2 = np.float32(math.log2(math.e) / math.sqrt(head_size))
    pipe = lax.axis_index("pipe")
    ctx = lax.axis_index("ctx")
    head = lax.axis_index("head")
    n_pipe = lax.axis_size("pipe")
    y = ctx // 2
    zh = ctx % 2

    def ring(step):
        return (pipe, ((y + step + NY) % NY) * 2 + zh, head)

    across = (pipe, y * 2 + (1 - zh), head)
    mate = y * 2 + (1 - zh)
    split_g = 2 + zh
    other_g = 3 - zh
    prev, following = (pipe + n_pipe - 1) % n_pipe, (pipe + 1) % n_pipe
    before, before_mate = (prev, ctx, head), (prev, mate, head)
    after, after_mate = (following, ctx, head), (following, mate, head)

    barrier = pltpu.get_barrier_semaphore()
    for other in (ring(1), ring(-1), across, before, after, before_mate, after_mate):
        pl.semaphore_signal(barrier, inc=1, device_id=other, device_id_type=MESH)

    loads = [
        pltpu.make_async_copy(src, dst, loc_sem.at[n])
        for n, (src, dst) in enumerate(((q_hbm, q_v), (g_hbm, g_v), (o_hbm, o_v)))
    ]
    for load in loads:
        load.start()

    for g in range(4):
        kv[ctx, g, 0] = (dot(kv_in[g, 0], had[...]) * inv).astype(BF16)
        kv[ctx, g, 1] = kv_in[g, 1]

    pl.semaphore_wait(barrier, 7)

    def block_of(half, i):
        sign = (1 - 2 * (i % 2)) * (1 - 2 * half)
        y_src = (y + sign * ((i + 1) // 2) + NY) % NY
        return y_src * 2 + (zh if half == 0 else 1 - zh)

    def kv_group(rg):
        return jnp.where(rg < 2, rg, split_g)

    def ag_copy(g, half, j, src, target):
        piece = kv.at[src, kv_group(g)]
        return pltpu.make_async_remote_copy(
            src_ref=piece, dst_ref=piece,
            send_sem=ag_send.at[g, half, j], recv_sem=ag_recv.at[g, half, j],
            device_id=target, device_id_type=MESH,
        )

    def z_copy(g, src):
        piece = kv.at[src, other_g if g == 2 else g]
        return pltpu.make_async_remote_copy(
            src_ref=piece, dst_ref=piece,
            send_sem=ag_send.at[g, 0, 0], recv_sem=ag_recv.at[g, 1, 0],
            device_id=across, device_id_type=MESH,
        )

    def ag_z(g):
        piece = kv.at[ctx, g]
        return pltpu.make_async_remote_copy(
            src_ref=piece, dst_ref=piece,
            send_sem=ag_send.at[g, 0, 0], recv_sem=ag_recv.at[g, 1, 0],
            device_id=across, device_id_type=MESH,
        )

    def row_copies():
        return [
            pltpu.make_async_remote_copy(
                src_ref=ref.at[4], dst_ref=ref.at[3],
                send_sem=row_send.at[n], recv_sem=row_recv.at[n],
                device_id=across, device_id_type=MESH,
            )
            for n, ref in enumerate((qr, gr, delta))
        ]

    def ag_event(half, e):
        pair, i = e // NY, e % NY
        lead = 1 - 2 * half
        src = block_of(half, i)

        def one(k, _):
            g = 2 * pair + k
            if half == 1:

                @pl.when(i == 0)
                def _():
                    ag_z(g).wait_recv()

            @pl.when(i > 0)
            def _():
                ag_copy(g, half, i, src, ring(1)).wait_recv()

            @pl.when(i == 0)
            def _():
                ag_copy(g, half, 1, src, ring(lead)).start()
                ag_copy(g, half, 2, src, ring(-lead)).start()

            @pl.when((i > 0) & (i <= 5))
            def _():
                way = lead * (2 * (i % 2) - 1)
                ag_copy(g, half, i + 2, src, ring(way)).start()

            return 0

        lax.fori_loop(0, 2 - pair, one, 0)

    def ag_step(u):
        @pl.when(u < 2 * NY)
        def _():
            ag_event(0, u)

        @pl.when((u >= LAG) & (u < LAG + 2 * NY))
        def _():
            ag_event(1, u - LAG)

        for g, when in enumerate(Z_STEPS):
            if when is not None:

                @pl.when(u == when)
                def _():
                    z_copy(g, ctx).start()

    for g, when in enumerate(Z_STEPS):
        if when is None:
            z_copy(g, ctx).start()

    m8[...] = jnp.full(m8.shape, NEG, F32)
    l8[...] = jnp.zeros(l8.shape, F32)
    zero_buf[...] = jnp.zeros(zero_buf.shape, BF16)
    row = lax.broadcasted_iota(jnp.int32, (8, 1024), 1)
    for n, block in enumerate((ctx, mate)):
        starts = jnp.where(row < 512, bo[2 * block], bo[2 * block + 1])
        qpos[n] = starts * 64 + ((row >> 3) & 63)

    def prep(j, _):
        toks = pl.ds(pl.multiple_of(j * 16, 16), 16)
        rows = pl.ds(pl.multiple_of(j * 128, 128), 128)
        q_c = q_v[toks].astype(F32)
        g_c = g_v[toks].astype(F32)
        o_c = o_v[toks].astype(F32)
        for g in range(4):
            hd = slice(8 * g, 8 * g + 8)
            to = g if g < 2 else jnp.where(g == split_g, 2, 4)
            q_g = q_c[:, hd, :].reshape(128, 128).astype(BF16)
            rot = dot(q_g, had[...]) * inv
            qr[to, rows, :] = rot.astype(BF16)
            qt[to, :, rows] = rot.T.astype(BF16)
            g_g = g_c[:, hd, :].reshape(128, 128)
            o_g = o_c[:, hd, :].reshape(128, 128)
            gr[to, rows, :] = g_g.astype(BF16)
            gt[to, :, rows] = g_g.T.astype(BF16)
            sums = jnp.sum((g_g * o_g).T, axis=0, keepdims=True)
            delta[to, :, rows] = jnp.broadcast_to(sums, (8, 128))
        return 0

    def warm(j, _):
        @pl.when(j < AHEAD)
        def _():
            ag_step(j)

        @pl.when(j == 0)
        def _():
            for load in loads:
                load.wait()

        prep(j, 0)
        return 0

    lax.fori_loop(0, 8, warm, 0)
    for copy in row_copies():
        copy.start()

    def take_rows():
        for copy in row_copies():
            copy.wait_recv()

        def turned(j, _):
            rows = pl.ds(pl.multiple_of(j * 128, 128), 128)
            qt[3, :, rows] = qr[3, rows, :].astype(F32).T.astype(BF16)
            gt[3, :, rows] = gr[3, rows, :].astype(F32).T.astype(BF16)
            return 0

        lax.fori_loop(0, 8, turned, 0)

    place = (
        lax.broadcasted_iota(jnp.int32, (8, 8, CHUNK), 0) * 8
        + lax.broadcasted_iota(jnp.int32, (8, 8, CHUNK), 1)
    )

    def stat_unit(g, i):
        blocks = (block_of(0, i), block_of(1, i))
        kg_at = kv_group(g)
        side = jnp.where(g == 3, 1, 0)
        k_two = jnp.concatenate([kv[blocks[0], kg_at, 0], kv[blocks[1], kg_at, 0]], axis=0)
        for c in range(1024 // CHUNK):
            cols = slice(c * CHUNK, (c + 1) * CHUNK)
            s = dot(k_two, qt[g, :, cols])
            q_at = qpos[side, :, cols]
            old = m8[g, :, cols]
            top = old
            parts = []
            for b in range(4):
                base = bo[2 * blocks[b // 2] + b % 2] * 64
                piece = s[64 * b : 64 * b + 64].reshape(8, 8, CHUNK) * to_log2
                piece = jnp.where(place <= (q_at - base)[None], piece, NEG)
                scores[g, blocks[b // 2], 64 * (b % 2) : 64 * (b % 2) + 64, cols] = piece.reshape(
                    64, CHUNK
                )
                top = jnp.maximum(top, jnp.max(piece, axis=0))
                parts.append(piece)
            run = l8[g, :, cols] * jnp.exp2(old - top)
            for piece in parts:
                run = run + jnp.sum(jnp.exp2(piece - top[None]), axis=0)
            m8[g, :, cols] = top
            l8[g, :, cols] = run

    def close_stats(g):
        top = jnp.max(m8[g], axis=0, keepdims=True)
        run = jnp.sum(l8[g] * jnp.exp2(m8[g] - top), axis=0, keepdims=True)
        lse[g] = jnp.broadcast_to(top + jnp.log2(run), (8, 1024))

    def rs_copy(g, j, d, target):
        return pltpu.make_async_remote_copy(
            src_ref=rs_out.at[g, j, d], dst_ref=rs_in.at[g, j, d],
            send_sem=rs_send.at[g, j, d], recv_sem=rs_recv.at[g, j, d],
            device_id=target, device_id_type=MESH,
        )

    def rs_z_copy(g):
        return pltpu.make_async_remote_copy(
            src_ref=rs_out.at[g, 7, :, pl.ds(0, 128)], dst_ref=rs_in.at[g, 7, :, pl.ds(0, 128)],
            send_sem=rs_send.at[g, 7, 0], recv_sem=rs_recv.at[g, 7, 0],
            device_id=across, device_id_type=MESH,
        )

    def hand_copy(g):
        return pltpu.make_async_remote_copy(
            src_ref=hs.at[g], dst_ref=hand.at[kv_group(g)],
            send_sem=h_send.at[g], recv_sem=h_recv.at[g],
            device_id=(prev, jnp.where(g == 3, mate, ctx), head), device_id_type=MESH,
        )

    def zero_copy(g):
        return pltpu.make_async_copy(zero_buf, hand.at[g], h_recv.at[g])

    def grad_unit(g, i):
        lead = jnp.where(g == 1, -1, 1)
        kg_at = kv_group(g)
        odd = i % 2
        sign = (2 * odd - 1) * lead
        y_dst = (y + sign * (4 - (i + 1) // 2) + NY) % NY
        first = 2 * y_dst
        k_two = jnp.concatenate([kv[first, kg_at, 0], kv[first + 1, kg_at, 0]], axis=0)
        v_two = jnp.concatenate([kv[first, kg_at, 1], kv[first + 1, kg_at, 1]], axis=0)

        k_t = k_two.T

        @pl.when(i == 0)
        def _():
            close_stats(g)
            dqt[g] = jnp.zeros((128, 1024), F32)

        for c in range(1024 // CHUNK):
            cols = slice(c * CHUNK, (c + 1) * CHUNK)
            dp = dot(v_two, gt[g, :, cols]).reshape(2, 16, 8, CHUNK)
            s = scores[g, pl.ds(first, 2), :, cols].reshape(2, 16, 8, CHUNK)
            p = jnp.exp2(s - lse[g, :, cols][None, None])
            ds = p * (dp - delta[g, :, cols][None, None])
            ds = ds.reshape(256, CHUNK).astype(BF16)
            ds_buf[:, cols] = ds
            pl_buf[:, cols] = p.reshape(256, CHUNK).astype(BF16)
        dqt[g] += dot(k_t, ds_buf[...])
        total[0] = dot(ds_buf[...], qr[g])
        total[1] = dot(pl_buf[...], gr[g])

        @pl.when(i == 7)
        def _():
            x = dqt[g] * inv
            a, b, c = split3(x)
            full = (dot(had[...], a) + dot(had[...], b) + dot(had[...], c)) * inv
            hs[g] = (full.T + gr[g].astype(F32)).astype(BF16)

            @pl.when(pipe > 0)
            def _():
                hand_copy(g).start()

        @pl.when(g == 3)
        def _():
            part[i] = total[...]

        @pl.when(g == 2)
        def _():
            total[...] += part[i]

        @pl.when(g < 3)
        def _():
            send_sums(g, i, sign)

    def send_sums(g, i, sign):
        for d in range(2):

            @pl.when(i < 2)
            def _():
                rs_out[g, i, d] = total[d].astype(BF16)

            @pl.when((i >= 2) & (i < 7))
            def _():
                rs_copy(g, i - 2, d, ring(1)).wait_recv()
                rs_out[g, i, d] = (total[d] + rs_in[g, i - 2, d].astype(F32)).astype(BF16)

            @pl.when(i < 7)
            def _():
                rs_copy(g, i, d, ring(sign)).start()

        @pl.when(i == 7)
        def _():
            for d in range(2):
                for j in (5, 6):
                    rs_copy(g, j, d, ring(1)).wait_recv()
            total[...] = total[...] + rs_in[g, 5].astype(F32) + rs_in[g, 6].astype(F32)
            theirs = pl.ds(pl.multiple_of((1 - zh) * 128, 128), 128)
            mine = pl.ds(pl.multiple_of(zh * 128, 128), 128)
            rs_out[g, 7, :, 0:128] = total[:, theirs].astype(BF16)
            rs_z_copy(g).start()
            fin[g] = total[:, mine]

    def put(g, both):
        a, b, c = split3(both[0] * inv)
        full = dot(a, had[...]) + dot(b, had[...]) + dot(c, had[...])
        kg[g] = (full * inv).astype(BF16)
        vg[g] = both[1].astype(BF16)

    def finish(g):
        rs_z_copy(g).wait_recv()
        theirs = rs_in[g, 7, :, 0:128].astype(F32)
        if g < 2:
            put(g, fin[g] + theirs)
        else:
            put(split_g, fin[g])
            put(other_g, theirs)

    def slot(t, _):
        turn, i = t // NY, t % NY

        ag_step(t + AHEAD)

        def stat(g, at):
            stat_unit(g, at)
            return 0

        @pl.when(turn == 0)
        def _():
            lax.fori_loop(0, 2, lambda k, _: stat(k, i), 0)

        @pl.when((turn == 1) & (i == ROWS_AT))
        def _():
            take_rows()

        @pl.when(turn == 1)
        def _():
            late = i - ROWS_AT
            many = jnp.where((late >= 0) & (late < 2), 5, 1)
            lax.fori_loop(
                0, many,
                lambda k, _: stat(jnp.where(k == 0, 2, 3), jnp.where(k == 0, i, 4 * late + k - 1)),
                0,
            )

        @pl.when(turn > 0)
        def _():
            early = i - (ROWS_AT + 2)
            many = jnp.where(
                turn == 1, jnp.where(early >= 0, 3, 1), jnp.where(i < REST, 3, 2)
            )

            def one(k, _):
                g = jnp.where(turn == 1, jnp.where(k == 0, 0, 3), 1 + k)
                at = jnp.where(
                    turn == 1,
                    jnp.where(k == 0, i, 2 * early + k - 1),
                    jnp.where(k == 2, NY - REST + i, i),
                )
                grad_unit(g, at)
                return 0

            lax.fori_loop(0, many, one, 0)

        @pl.when(t == 2 * NY + 2)
        def _():
            finish(0)

        return 0

    lax.fori_loop(0, 3 * NY, slot, 0)

    @pl.when(pipe == n_pipe - 1)
    def _():
        for g in range(4):
            zero_copy(g).start()

    for g in range(1, 3):
        finish(g)

    @pl.when(pipe == n_pipe - 1)
    def _():
        for g in range(4):
            zero_copy(g).wait()

    @pl.when(pipe < n_pipe - 1)
    def _():
        for g in range(4):
            hand_copy(g).wait_recv()

    @pl.when(pipe > 0)
    def _():
        for g in range(4):
            hand_copy(g).wait_send()

    for copy in row_copies():
        copy.wait_send()
    for g in range(3):
        z_copy(g, ctx).wait_send()
        for half in range(2):
            for j in range(1, 8):
                ag_copy(g, half, j, ctx, ring(1)).wait_send()
        for j in range(7):
            for d in range(2):
                rs_copy(g, j, d, ring(1)).wait_send()
        rs_z_copy(g).wait_send()


def shards(queries, key_heads, value_heads, forward_out, output_grad, block_order):
    tok = queries.shape[1]
    kv_in = jnp.stack([key_heads[0], value_heads[0]]).transpose(2, 0, 1, 3)
    had = jnp.asarray(signs(128), BF16)
    vmem = pl.BlockSpec(memory_space=pltpu.VMEM)
    hbm = pl.BlockSpec(memory_space=pl.ANY)
    dma = pltpu.SemaphoreType.DMA
    kg, vg, hand = pl.pallas_call(
        kernel,
        out_shape=(
            jax.ShapeDtypeStruct((4, tok, 128), BF16),
            jax.ShapeDtypeStruct((4, tok, 128), BF16),
            jax.ShapeDtypeStruct((4, 8 * tok, 128), BF16),
        ),
        in_specs=[pl.BlockSpec(memory_space=pltpu.SMEM), vmem, vmem, hbm, hbm, hbm],
        out_specs=(vmem, vmem, hbm),
        scratch_shapes=[
            pltpu.VMEM((tok, 32, 128), BF16),
            pltpu.VMEM((tok, 32, 128), BF16),
            pltpu.VMEM((tok, 32, 128), BF16),
            pltpu.VMEM((16, 4, 2, 128, 128), BF16),
            pltpu.VMEM((5, 1024, 128), BF16),
            pltpu.VMEM((5, 128, 1024), BF16),
            pltpu.VMEM((5, 1024, 128), BF16),
            pltpu.VMEM((5, 128, 1024), BF16),
            pltpu.VMEM((5, 8, 1024), F32),
            pltpu.VMEM((2, 8, 1024), jnp.int32),
            pltpu.VMEM((4, 8, 1024), F32),
            pltpu.VMEM((4, 8, 1024), F32),
            pltpu.VMEM((4, 8, 1024), F32),
            pltpu.VMEM((4, 16, 128, 1024), F32),
            pltpu.VMEM((256, 1024), BF16),
            pltpu.VMEM((256, 1024), BF16),
            pltpu.VMEM((4, 128, 1024), F32),
            pltpu.VMEM((3, 8, 2, 256, 128), BF16),
            pltpu.VMEM((3, 8, 2, 256, 128), BF16),
            pltpu.VMEM((8, 2, 256, 128), F32),
            pltpu.VMEM((2, 256, 128), F32),
            pltpu.VMEM((3, 2, 128, 128), F32),
            pltpu.VMEM((4, 1024, 128), BF16),
            pltpu.VMEM((1024, 128), BF16),
            dma((3,)),
            dma((3,)),
            dma((3,)),
            dma((3, 2, 8)),
            dma((3, 2, 8)),
            dma((3, 8, 2)),
            dma((3, 8, 2)),
            dma((4,)),
            dma((4,)),
        ],
        compiler_params=pltpu.CompilerParams(
            collective_id=0, has_side_effects=True, vmem_limit_bytes=60 * 1024 * 1024
        ),
        cost_estimate=pl.CostEstimate(
            flops=11_000_000_000, bytes_accessed=5_000_000, transcendentals=17_000_000
        ),
    )(block_order, kv_in, had, queries[0], output_grad[0], forward_out[0])
    key_grad = kg.transpose(1, 0, 2)[None]
    value_grad = vg.transpose(1, 0, 2)[None]
    handed = hand.reshape(4, tok, 8, 128).transpose(1, 0, 2, 3).reshape(1, tok, 32, 128)
    return (key_grad, value_grad, handed)


def solution(mesh):
    placed = P("pipe", "ctx", "head", None)
    return jax.shard_map(
        shards,
        mesh=mesh,
        in_specs=(placed,) * 5 + (P(),),
        out_specs=(placed,) * 3,
        check_vma=False,
    )
```

time: 135 us -> 120 us (0.89)
  the two profiles are of different devices: /device:TPU:134 before, /device:TPU:192 now
where the time goes in v2:
time: 120 us; the launch traced here: 119 us
  Pallas kernels  112 us (93%)
  local copies, waits for them, and re-layouts  5.82 us (5%)
    pallas_call x1, Pallas kernels, shards(): pl.pallas_call(kernel, out_shape=(jax.ShapeDtypeStruct((4, tok, 128), BF1...  112 us
    unnamed x8, local copies, waits for them, and re-layouts  3.44 us

profile of v2, /device:TPU:192, one launch (start us, length us, event | category | flops | bytes accessed | tf_op | source)
XLA Modules:
  0.0 119.4 jit_solution(14439232499581863092)
XLA Ops:
  0.6 0.0 copy-start
  0.6 1.0 copy.10
  1.6 0.0 copy-done
  1.6 0.7 maximum_bitcast_fusion.kv_in
  2.4 112.1 %shard_map.94 = (bf16[4,128,128]{2,1,0:T(8,128)(2,1)}, bf16[4,128,128]{2,1,0:T(8,128)(2,1)}, bf16[4,1024,128]{2,1,0:T(8,128)(2,1)}) custom-call(s32[32]{0:T(128)} %bo.1, bf16[4,2,128,128]{3,2,1,0:T(8,128)(2,1)} %maximum_bitcast_fusion.kv_in, bf16[128,128]{1,0:T(8,128)(2,1)} %constant.2.clone.had, bf16[128,32,128]{2,1,0:T(8,128)(2,1)} %bitcast.20, ...), custom_call_target="tpu_custom_call" | custom-call | flops 11000000512 | bytes 5000000 | tf_op jit(solution)/shard_map/pallas_call | solution.py:495
  114.5 0.0 copy-start.1
  114.5 1.7 %copy.13 = bf16[1,128,4,128]{3,2,1,0:T(4,128)(2,1)} copy(bf16[1,128,4,128]{3,1,2,0:T(8,128)(2,1)} %bitcast.19) | data formatting | bytes 262144
  116.2 0.0 copy-done.1
  116.2 0.8 copy.14
  117.0 2.4 %copy_bitcast_fusion = bf16[1,128,32,128]{3,2,1,0:T(8,128)(2,1)} fusion(bf16[4,1024,128]{2,1,0:T(8,128)(2,1)} %get-tuple-element.8), kind=kLoop, calls=%fused_computation | loop fusion | bytes 2097152 | tf_op jit(solution)/shard_map/reshape | solution.py:548
  (1 shorter events, 0.0 us)
Async XLA Ops:
  0.6 1.0 copy-start
  114.5 1.7 %copy-start.1 = (bf16[4,128,128]{2,1,0:T(8,128)(2,1)S(1)}, bf16[4,128,128]{2,1,0:T(8,128)(2,1)}, u32[]{:S(2)}) copy-start(bf16[4,128,128]{2,1,0:T(8,128)(2,1)} %get-tuple-element.7) | copy-start | bytes 393220

commit v3 on v2

--- a/solution.py
+++ b/solution.py
@@ -15,9 +15,9 @@
 NY = 8
 ROWS_AT = 4
 REST = 8 - 2 * (NY - ROWS_AT - 2)
-LAG = 2
-AHEAD = LAG + 2
-Z_STEPS = (None, None, 3)
+LAG = 1
+AHEAD = LAG + 3
+Z_STEPS = (None, None, 2)
 CHUNK = 512
 
 
@@ -43,7 +43,7 @@
 
 
 def kernel(
-    bo, kv_in, had, q_hbm, g_hbm, o_hbm,
+    bo, k_in, v_in, had, q_hbm, g_hbm, o_hbm,
     kg, vg, hand,
     q_v, g_v, o_v, kv, qr, qt, gr, gt, delta, qpos, m8, l8, lse, scores, ds_buf, pl_buf, dqt,
     rs_out, rs_in, part, total, fin, hs, zero_buf,
@@ -82,8 +82,8 @@
         load.start()
 
     for g in range(4):
-        kv[ctx, g, 0] = (dot(kv_in[g, 0], had[...]) * inv).astype(BF16)
-        kv[ctx, g, 1] = kv_in[g, 1]
+        kv[ctx, g, 0] = (dot(k_in[g], had[...]) * inv).astype(BF16)
+        kv[ctx, g, 1] = v_in[g]
 
     pl.semaphore_wait(barrier, 7)
 
@@ -160,14 +160,15 @@
 
         lax.fori_loop(0, 2 - pair, one, 0)
 
-    def ag_step(u):
+    def ag_mate(u):
+        @pl.when((u >= LAG) & (u < LAG + 2 * NY))
+        def _():
+            ag_event(1, u - LAG)
+
+    def ag_own(u):
         @pl.when(u < 2 * NY)
         def _():
             ag_event(0, u)
-
-        @pl.when((u >= LAG) & (u < LAG + 2 * NY))
-        def _():
-            ag_event(1, u - LAG)
 
         for g, when in enumerate(Z_STEPS):
             if when is not None:
@@ -212,7 +213,8 @@
     def warm(j, _):
         @pl.when(j < AHEAD)
         def _():
-            ag_step(j)
+            ag_own(j)
+            ag_mate(j)
 
         @pl.when(j == 0)
         def _():
@@ -398,7 +400,7 @@
     def slot(t, _):
         turn, i = t // NY, t % NY
 
-        ag_step(t + AHEAD)
+        ag_own(t + AHEAD)
 
         def stat(g, at):
             stat_unit(g, at)
@@ -421,6 +423,8 @@
                 lambda k, _: stat(jnp.where(k == 0, 2, 3), jnp.where(k == 0, i, 4 * late + k - 1)),
                 0,
             )
+
+        ag_mate(t + AHEAD)
 
         @pl.when(turn > 0)
         def _():
@@ -487,7 +491,8 @@
 
 def shards(queries, key_heads, value_heads, forward_out, output_grad, block_order):
     tok = queries.shape[1]
-    kv_in = jnp.stack([key_heads[0], value_heads[0]]).transpose(2, 0, 1, 3)
+    k_in = key_heads[0].transpose(1, 0, 2)
+    v_in = value_heads[0].transpose(1, 0, 2)
     had = jnp.asarray(signs(128), BF16)
     vmem = pl.BlockSpec(memory_space=pltpu.VMEM)
     hbm = pl.BlockSpec(memory_space=pl.ANY)
@@ -499,7 +504,7 @@
             jax.ShapeDtypeStruct((4, tok, 128), BF16),
             jax.ShapeDtypeStruct((4, 8 * tok, 128), BF16),
         ),
-        in_specs=[pl.BlockSpec(memory_space=pltpu.SMEM), vmem, vmem, hbm, hbm, hbm],
+        in_specs=[pl.BlockSpec(memory_space=pltpu.SMEM), vmem, vmem, vmem, hbm, hbm, hbm],
         out_specs=(vmem, vmem, hbm),
         scratch_shapes=[
             pltpu.VMEM((tok, 32, 128), BF16),
@@ -542,7 +547,7 @@
         cost_estimate=pl.CostEstimate(
             flops=11_000_000_000, bytes_accessed=5_000_000, transcendentals=17_000_000
         ),
-    )(block_order, kv_in, had, queries[0], output_grad[0], forward_out[0])
+    )(block_order, k_in, v_in, had, queries[0], output_grad[0], forward_out[0])
     key_grad = kg.transpose(1, 0, 2)[None]
     value_grad = vg.transpose(1, 0, 2)[None]
     handed = hand.reshape(4, tok, 8, 128).transpose(1, 0, 2, 3).reshape(1, tok, 32, 128)

time: 120 us -> 121 us (level)
  Pallas kernels: 112 us -> 114 us
    transpose x0 -> x1, local copies, waits for them, and re-layouts: none -> 1.7 us  [shards(): v_in = value_heads[0].transpose(1, 0, 2)]
    pallas_call x1, Pallas kernels: 112 us -> 114 us  [shards(): pl.pallas_call(kernel, out_shape=(jax.ShapeDtypeStruct((4, tok, 128), BF1...]
    unnamed x8 -> x4, local copies, waits for them, and re-layouts: 3.44 us -> 2.46 us
where the time goes in v3:
time: 121 us
  Pallas kernels  114 us (94%)
  local copies, waits for them, and re-layouts  6.54 us (5%)
    pallas_call x1, Pallas kernels, shards(): pl.pallas_call(kernel, out_shape=(jax.ShapeDtypeStruct((4, tok, 128), BF1...  114 us
    unnamed x4, local copies, waits for them, and re-layouts  2.46 us

profile of v3, /device:TPU:192, one launch (start us, length us, event | category | flops | bytes accessed | tf_op | source)
XLA Modules:
  0.0 120.9 jit_solution(13817560655032615884)
XLA Ops:
  0.6 1.7 %copy_bitcast_fusion.1 = (bf16[4,128,128]{2,1,0:T(8,128)(2,1)}, bf16[4,128,128]{2,1,0:T(8,128)(2,1)}) fusion(bf16[1,128,4,128]{3,2,1,0:T(4,128)(2,1)} %param.9, bf16[1,128,4,128]{3,2,1,0:T(4,128)(2,1)} %param.8), kind=kLoop, calls=%fused_computation.1 | loop fusion | bytes 524288 | tf_op jit(solution)/shard_map/transpose | solution.py:495
  2.3 113.8 %shard_map.94 = (bf16[4,128,128]{2,1,0:T(8,128)(2,1)}, bf16[4,128,128]{2,1,0:T(8,128)(2,1)}, bf16[4,1024,128]{2,1,0:T(8,128)(2,1)}) custom-call(s32[32]{0:T(128)} %bo.1, bf16[4,128,128]{2,1,0:T(8,128)(2,1)} %get-tuple-element.13.k_in, bf16[4,128,128]{2,1,0:T(8,128)(2,1)} %get-tuple-element.12.v_in, bf16[128,128]{1,0:T(8,128)(2,1)} %constant.2.clone.had, ...), custom_call_target="tpu_custom_call" | custom-call | flops 11000000512 | bytes 5000000 | tf_op jit(solution)/shard_map/pallas_call | solution.py:500
  116.1 0.0 copy-start
  116.1 1.7 %copy.13 = bf16[1,128,4,128]{3,2,1,0:T(4,128)(2,1)} copy(bf16[1,128,4,128]{3,1,2,0:T(8,128)(2,1)} %bitcast.25) | data formatting | bytes 262144
  117.8 0.0 copy-done
  117.8 0.8 copy.14
  118.6 2.4 %copy_bitcast_fusion = bf16[1,128,32,128]{3,2,1,0:T(8,128)(2,1)} fusion(bf16[4,1024,128]{2,1,0:T(8,128)(2,1)} %get-tuple-element.8), kind=kLoop, calls=%fused_computation | loop fusion | bytes 2097152 | tf_op jit(solution)/shard_map/reshape | solution.py:553
Async XLA Ops:
  116.1 1.7 %copy-start = (bf16[4,128,128]{2,1,0:T(8,128)(2,1)S(1)}, bf16[4,128,128]{2,1,0:T(8,128)(2,1)}, u32[]{:S(2)}) copy-start(bf16[4,128,128]{2,1,0:T(8,128)(2,1)} %get-tuple-element.7) | copy-start | bytes 393220
